TPU v7x, 256 devices: a whole 4x4x8 slice. The times are simulated.
256 devices in a mesh: row: 32 (over y, z), col: 8 (over x, core).
Axes of the slice: x: 4, y: 4, z: 8, core: 2. Of those that a mesh axis runs over, the one named last changes fastest.
Arguments:
- homolog_embedding: bfloat16 [32, 1024, 256], P('col', 'row'), may hold values from -6 to 6
- standardize_factor: float32 [256], replicated, may hold values from 0.25 to 1.75
- standardize_shift: float32 [256], replicated, may hold values from -3 to 3
- embed_matrices: bfloat16 [256, 64], replicated, may hold values from -0.375 to 0.375
- embed_shifts: float32 [64], replicated, may hold values from -4 to 4
- final_matrix: bfloat16 [1024, 128], replicated, may hold values from -0.1875 to 0.1875
- final_shift: float32 [128], replicated, may hold values from -4 to 4
- contact_update_cotangent: bfloat16 [1024, 1024, 128], P('row', 'col'), may hold values from -6 to 6
Outputs:
- pair_update: bfloat16 [1024, 1024, 128], P('row', 'col')
- alignment_gradient: float32 [32, 1024, 256], P('col', 'row')
- out_weight_grad: float32 [1024, 128], replicated
- proj_weight_grad: float32 [256, 64], replicated
All inputs are finite; a program needn't handle non-finite values.
Results may differ from a plain program's by a relative error of at most 0.019.
Values may be sent and summed in bfloat16 or wider, within the bound.
A program may use at most 64 MiB of HBM per device.

v0:
```python
import jax
import jax.numpy as jnp
from jax import lax
from jax.sharding import PartitionSpec as P


def from_root(block, axis, source):
    block = jnp.where(lax.axis_index(axis) == source, block, jnp.zeros_like(block))
    return lax.psum(block, axis)


def standardized_blocks(homolog_embedding, standardize_factor, standardize_shift):
    tensor_product_entries = homolog_embedding.astype(jnp.float32)
    centre = tensor_product_entries - jnp.mean(tensor_product_entries, axis=-1, keepdims=True)
    reciprocal_spread = lax.rsqrt(jnp.mean(centre * centre, axis=-1, keepdims=True) + 1e-05)
    centred_features = centre * reciprocal_spread
    standardized_matrix = (centred_features * standardize_factor + standardize_shift).astype(
        jnp.bfloat16
    )
    return (centred_features, reciprocal_spread, standardized_matrix)


def pair_blocks(a_flat, b_flat, final_matrix, final_shift, cotangent, width):
    seqs = a_flat.shape[0]
    rows, cols, pair_ch = cotangent.shape
    step = 8
    inv_seq = 1.0 / seqs

    def one_block(carry, index):
        weight_gradient, dbsum = carry
        a_block = lax.dynamic_slice_in_dim(a_flat, index * (step * width), step * width, 1)
        outer = lax.dot_general(
            a_block, b_flat, (((0,), (0,)), ((), ())), preferred_element_type=jnp.float32
        )
        outer = (
            outer.reshape(step, width, cols, width)
            .transpose(0, 2, 1, 3)
            .reshape(step * cols, width * width)
        )
        outer = (outer * inv_seq).astype(jnp.bfloat16)
        grad_rows = lax.dynamic_slice_in_dim(cotangent, index * step, step, 0).reshape(
            step * cols, pair_ch
        )
        update = (
            jnp.dot(outer, final_matrix, preferred_element_type=jnp.float32) + final_shift
        ).astype(jnp.bfloat16)
        douter = lax.dot_general(
            grad_rows, final_matrix, (((1,), (1,)), ((), ())), preferred_element_type=jnp.float32
        ).astype(jnp.bfloat16)
        weight_gradient = weight_gradient + lax.dot_general(
            outer, grad_rows, (((0,), (0,)), ((), ())), preferred_element_type=jnp.float32
        )
        dmixed = (
            douter.reshape(step, cols, width, width)
            .transpose(0, 2, 1, 3)
            .reshape(step * width, cols * width)
        )
        da_block = (
            lax.dot_general(
                b_flat, dmixed, (((1,), (1,)), ((), ())), preferred_element_type=jnp.float32
            )
            * inv_seq
        )
        dbsum = dbsum + jnp.dot(a_block, dmixed, preferred_element_type=jnp.float32)
        return ((weight_gradient, dbsum), (update.reshape(step, cols, pair_ch), da_block))

    start = (
        jnp.zeros((width * width, pair_ch), jnp.float32),
        jnp.zeros((seqs, cols * width), jnp.float32),
    )
    indices = jnp.arange(rows // step, dtype=jnp.int32)
    (weight_gradient, dbsum), (updates, da_blocks) = lax.scan(one_block, start, indices)
    pair_state = updates.reshape(rows, cols, pair_ch)
    da_flat = da_blocks.transpose(1, 0, 2).reshape(seqs, rows * width)
    return (pair_state, da_flat, dbsum * inv_seq, weight_gradient)


def norm_gradient_pass(
    projection_gradient,
    centred_features,
    reciprocal_spread,
    standardized_matrix,
    standardize_factor,
    embed_matrices,
):
    feature_number = standardized_matrix.shape[-1]
    weight_wide = embed_matrices.astype(jnp.float32)
    pair_gradient = jnp.dot(
        standardized_matrix.astype(jnp.float32).reshape(-1, feature_number).T,
        projection_gradient.reshape(-1, projection_gradient.shape[-1]),
        precision=lax.Precision.HIGHEST,
    )
    dnorm = (
        jnp.dot(projection_gradient, weight_wide.T, precision=lax.Precision.HIGHEST)
        * standardize_factor
    )
    mean_one = jnp.mean(dnorm, axis=-1, keepdims=True)
    mean_two = jnp.mean(dnorm * centred_features, axis=-1, keepdims=True)
    return (reciprocal_spread * (dnorm - mean_one - centred_features * mean_two), pair_gradient)


def on_device(
    homolog_embedding,
    standardize_factor,
    standardize_shift,
    embed_matrices,
    embed_shifts,
    final_matrix,
    final_shift,
    contact_update_cotangent,
):
    homolog_shard_lines, amino_shard_lines, feature_number = homolog_embedding.shape
    width = embed_matrices.shape[1] // 2
    col_count = lax.axis_size("col")
    ratio = lax.axis_size("row") // col_count
    residues = amino_shard_lines * lax.axis_size("row")
    col_index = lax.axis_index("col")
    row_index = lax.axis_index("row")
    centred_features, reciprocal_spread, standardized_matrix = standardized_blocks(
        homolog_embedding, standardize_factor, standardize_shift
    )
    proj = (
        jnp.dot(standardized_matrix, embed_matrices, preferred_element_type=jnp.float32)
        + embed_shifts
    ).astype(jnp.bfloat16)
    packed = jnp.concatenate(
        [
            proj[..., :width].reshape(homolog_shard_lines, amino_shard_lines * width),
            proj[..., width:].reshape(homolog_shard_lines, amino_shard_lines * width),
        ],
        axis=1,
    )
    all_seqs = lax.all_gather(packed, "col", axis=0, tiled=True)
    a_flat = all_seqs[:, : amino_shard_lines * width]
    b_local = all_seqs[:, amino_shard_lines * width :]
    b_whole = lax.all_gather(b_local, "row", axis=1, tiled=True)
    b_flat = lax.dynamic_slice_in_dim(
        b_whole,
        col_index * (ratio * amino_shard_lines * width),
        ratio * amino_shard_lines * width,
        1,
    )
    pair_state, da_part, db_part, weight_gradient = pair_blocks(
        a_flat, b_flat, final_matrix, final_shift, contact_update_cotangent, width
    )
    da_own = lax.psum_scatter(
        da_part.astype(jnp.bfloat16), "col", scatter_dimension=0, tiled=True
    ).astype(jnp.float32)
    db_block = lax.psum(db_part.astype(jnp.bfloat16), "row").astype(jnp.float32)
    db_piece = lax.dynamic_slice_in_dim(
        db_block, row_index % ratio * (amino_shard_lines * width), amino_shard_lines * width, 1
    )
    db_rows = from_root(db_piece.astype(jnp.bfloat16), "col", row_index // ratio).astype(
        db_piece.dtype
    )
    db_own = lax.dynamic_slice_in_dim(
        db_rows, col_index * homolog_shard_lines, homolog_shard_lines, 0
    )
    projection_gradient = jnp.concatenate(
        [
            da_own.reshape(homolog_shard_lines, amino_shard_lines, width),
            db_own.reshape(homolog_shard_lines, amino_shard_lines, width),
        ],
        axis=-1,
    )
    alignment_gradient, pair_gradient = norm_gradient_pass(
        projection_gradient,
        centred_features,
        reciprocal_spread,
        standardized_matrix,
        standardize_factor,
        embed_matrices,
    )
    weight_gradient_sum, device_total_sum = lax.psum(
        (weight_gradient, pair_gradient), ("row", "col")
    )
    sequence_scale = 1.0 / residues
    return (
        pair_state,
        alignment_gradient,
        weight_gradient_sum * sequence_scale,
        device_total_sum * sequence_scale,
    )


def solution(mesh):
    in_specs = (P("col", "row", None), P(), P(), P(), P(), P(), P(), P("row", "col", None))
    out_specs = (P("row", "col", None), P("col", "row", None), P(), P())
    return jax.shard_map(
        on_device, mesh=mesh, in_specs=in_specs, out_specs=out_specs, check_vma=False
    )
```

profile of v0, /device:TPU:1, one launch (start us, length us, event | category | flops | bytes accessed | tf_op | source)
XLA Modules:
  0.0 773.7 jit_solution(5773870534078878079)
XLA Ops:
  10.6 15.8 %all-gather = bf16[8,4,2048]{2,1,0:T(4,128)(2,1)S(1)} all-gather(bf16[1,4,2048]{2,1,0:T(4,128)(2,1)S(1)} %maximum_bitcast_fusion), channel_id=1, replica_groups=mesh['row'=32,'col'=8] {'col'}, dimensions={0}, use_global_device_ids=true | all-gather | bytes 147456 | tf_op jit(solution)/shard_map/all_gather | solution.py:133
  27.2 74.6 %all-gather.3.cloned.1.call-done = bf16[32,32768]{1,0:T(8,128)(2,1)} async-done(((bf16[32,1024]{1,0:T(8,128)(2,1)}), bf16[32,32768]{1,0:T(8,128)(2,1)}) %all-gather.3.cloned.1.call-update) | async-done | bytes 2097168 | tf_op jit(solution)/shard_map/all_gather | solution.py:136
  102.8 194.6 %while.17 = (s32[]{:T(128)}, f32[1024,128]{1,0:T(8,128)}, f32[32,4096]{1,0:T(8,128)S(1)}, bf16[4,8,128,128]{3,2,1,0:T(8,128)(2,1)}, bf16[4,32,256]{2,1,0:T(8,128...) while((s32[]{:T(128)}, f32[1024,128]{1,0:T(8,128)}, ...), condition=%wide.region_3.4_spmd.clone, body=%wide.region_2.3_spmd.clone.sunk | while | flops 1010573312 | bytes 61148112 | solution.py:72
  107.2 8.1 %convert_element_type.119 = bf16[8,32,128,32]{3,2,1,0:T(8,128)(2,1)} reshape(bf16[256,4096]{1,0:T(8,128)(2,1)S(1)} %fusion.80) | data formatting | bytes 4194304 | tf_op jit(solution)/shard_map/while/body/eval_jaxpr/convert_element_type | solution.py:40
  115.2 6.9 copy.45
  124.4 2.6 copy.46
  127.0 2.2 copy.47
  129.2 5.9 copy.48
  135.2 10.7 %reshape.99 = bf16[256,4096]{1,0:T(8,128)(2,1)S(1)} reshape(bf16[8,32,128,32]{3,2,1,0:T(8,128)(2,1)} %copy.48) | data formatting | bytes 4194304 | tf_op jit(solution)/shard_map/while/body/eval_jaxpr/reshape | solution.py:56
  154.6 8.1 %convert_element_type.119 = bf16[8,32,128,32]{3,2,1,0:T(8,128)(2,1)} reshape(bf16[256,4096]{1,0:T(8,128)(2,1)S(1)} %fusion.80) | data formatting | bytes 4194304 | tf_op jit(solution)/shard_map/while/body/eval_jaxpr/convert_element_type | solution.py:40
  162.7 6.9 copy.45
  169.7 3.1 fusion.81
  173.5 2.6 copy.46
  176.0 2.2 copy.47
  178.3 5.9 copy.48
  184.2 10.7 %reshape.99 = bf16[256,4096]{1,0:T(8,128)(2,1)S(1)} reshape(bf16[8,32,128,32]{3,2,1,0:T(8,128)(2,1)} %copy.48) | data formatting | bytes 4194304 | tf_op jit(solution)/shard_map/while/body/eval_jaxpr/reshape | solution.py:56
  203.7 8.1 %convert_element_type.119 = bf16[8,32,128,32]{3,2,1,0:T(8,128)(2,1)} reshape(bf16[256,4096]{1,0:T(8,128)(2,1)S(1)} %fusion.80) | data formatting | bytes 4194304 | tf_op jit(solution)/shard_map/while/body/eval_jaxpr/convert_element_type | solution.py:40
  211.7 6.9 copy.45
  218.7 3.1 fusion.81
  222.5 2.6 copy.46
  225.1 2.2 copy.47
  227.3 5.9 copy.48
  233.2 10.7 %reshape.99 = bf16[256,4096]{1,0:T(8,128)(2,1)S(1)} reshape(bf16[8,32,128,32]{3,2,1,0:T(8,128)(2,1)} %copy.48) | data formatting | bytes 4194304 | tf_op jit(solution)/shard_map/while/body/eval_jaxpr/reshape | solution.py:56
  252.7 8.1 %convert_element_type.119 = bf16[8,32,128,32]{3,2,1,0:T(8,128)(2,1)} reshape(bf16[256,4096]{1,0:T(8,128)(2,1)S(1)} %fusion.80) | data formatting | bytes 4194304 | tf_op jit(solution)/shard_map/while/body/eval_jaxpr/convert_element_type | solution.py:40
  260.8 6.9 copy.45
  267.7 3.1 fusion.81
  271.5 2.6 copy.46
  276.3 5.9 copy.48
  282.3 10.7 %reshape.99 = bf16[256,4096]{1,0:T(8,128)(2,1)S(1)} reshape(bf16[8,32,128,32]{3,2,1,0:T(8,128)(2,1)} %copy.48) | data formatting | bytes 4194304 | tf_op jit(solution)/shard_map/while/body/eval_jaxpr/reshape | solution.py:56
  299.7 139.5 %all-reduce.7.cloned.1.call-done = bf16[32,4096]{1,0:T(8,128)(2,1)} async-done(((bf16[32,4096]{1,0:T(8,128)(2,1)}), bf16[32,4096]{1,0:T(8,128)(2,1)}) %all-reduce.7.cloned.1.call-update) | async-done | bytes 262160 | tf_op jit(solution)/shard_map/psum | solution.py:149
  442.1 63.9 %all-reduce.11.cloned.1.call-done = (bf16[32,1024]{1,0:T(8,128)(2,1)}, bf16[32,1024]{1,0:T(8,128)(2,1)}) async-done(((bf16[32,1024]{1,0:T(8,128)(2,1)}, bf16[32,1024]{1,0:T(8,128)(2,1)}), (bf16[32,1024]{1,0:T(8,128)(2,1)}, bf16[32,1024]{1,0:T(8,128)(2,1)})) %all-reduce.11.cloned.1.call-update) | async-done | bytes 131088 | tf_op jit(solution)/shard_map/psum | solution.py:9
  509.1 254.8 %all-reduce.9.cloned.1.call-done = (f32[1024,128]{1,0:T(8,128)}, f32[256,64]{0,1:T(8,128)}) async-done(((f32[1024,128]{1,0:T(8,128)}, f32[256,64]{0,1:T(8,128)}), (f32[1024,128]{1,0:T(8,128)}, f32[256,64]{0,1:T(8,128)})) %all-reduce.9.cloned.1.call-update) | async-done | bytes 589840 | tf_op jit(solution)/shard_map/psum | solution.py:174
  (131 shorter events, 52.3 us)
Async XLA Ops:
  7.2 2.0 copy-start
  7.2 94.6 %all-gather.3.cloned.1.call-start = ((), (), s32[]{:S(2)}) async-start(), calls=%async_computation | async-start | bytes 2162688 | tf_op jit(solution)/shard_map/all_gather | solution.py:136
  27.1 412.1 %all-reduce.7.cloned.1.call-start = ((), (), s32[]{:S(2)}) async-start(), calls=%async_computation.1 | async-start | bytes 524288 | tf_op jit(solution)/shard_map/psum | solution.py:149
  102.8 338.0 %copy-start.10 = (u32[256]{0:T(256)S(1)}, u32[256]{0:T(256)}, u32[]{:S(2)}) copy-start(u32[256]{0:T(256)} %constant.91) | copy-start | bytes 3076
  102.8 404.1 %copy-start.4 = (bf16[4,32,256]{2,1,0:T(8,128)(2,1)S(1)}, bf16[4,32,256]{2,1,0:T(8,128)(2,1)}, u32[]{:S(2)}) copy-start(bf16[4,32,256]{2,1,0:T(8,128)(2,1)} %param.10) | copy-start | bytes 196612
  102.8 404.1 %copy-start.7 = (f32[256]{0:T(256)S(1)}, f32[256]{0:T(256)}, u32[]{:S(2)}) copy-start(f32[256]{0:T(256)} %param.11) | copy-start | bytes 3076
  122.2 1.6 copy-start.1
  122.2 1.5 copy-start.3
  145.8 1.6 copy-start.2
  145.8 1.6 copy-start.9
  147.4 1.5 copy-start.5
  149.7 0.6 copy-start.6
  169.6 3.1 copy-start.1
  169.7 3.1 copy-start.3
  194.9 1.6 copy-start.2
  194.9 1.6 copy-start.9
  196.5 1.5 copy-start.5
  198.7 0.6 copy-start.6
  218.7 3.1 copy-start.1
  218.7 3.1 copy-start.3
  243.9 1.6 copy-start.2
  243.9 1.6 copy-start.9
  245.5 1.5 copy-start.5
  267.7 3.1 copy-start.1
  267.7 3.1 copy-start.3
  292.9 1.6 copy-start.2
  292.9 1.6 copy-start.9
  294.5 1.5 copy-start.5
  296.8 0.6 copy-start.6
  297.4 209.9 %copy-start.8 = (f32[256]{0:T(256)S(1)}, f32[256]{0:T(256)}, u32[]{:S(2)}) copy-start(f32[256]{0:T(256)} %param.12) | copy-start | bytes 3076
  298.2 207.8 %all-reduce.11.cloned.1.call-start = ((), (), s32[]{:S(2)}) async-start(), calls=%async_computation.3 | async-start | bytes 262144 | tf_op jit(solution)/shard_map/psum | solution.py:9
  440.7 323.1 %all-reduce.9.cloned.1.call-start = ((), (), s32[]{:S(2)}) async-start(), calls=%async_computation.2 | async-start | bytes 1179648 | tf_op jit(solution)/shard_map/psum | solution.py:174
  (1 other events, 0.6 us)
Sparse Core Ops, SparseCore 0:
  27.3 74.4 all-gather.2
  298.3 140.8 all-reduce.6
  442.2 63.7 all-reduce.10
  512.9 250.8 all-reduce.8
where the time goes:
time: 776 us; the launch traced here: 774 us
  waiting for transfers between devices  533 us (69%)
  local copies, waits for them, and re-layouts  162 us (21%)
  matrix products  33.1 us (4%)
  blocking collectives  15.8 us (2%)
  between operations  14.7 us (2%)
  other arithmetic  9.07 us (1%)
    psum x1, waiting for transfers between devices, on_device(): lax.psum((weight_gradient, pair_gradient), ('row', 'col'))  255 us
    psum x1, waiting for transfers between devices, on_device(): db_block = lax.psum(db_part.astype(jnp.bfloat16), 'row').astype(jnp.float32)  139 us
    all_gather x1, waiting for transfers between devices, on_device(): b_whole = lax.all_gather(b_local, 'row', axis=1, tiled=True)  74.6 us
    psum x1, waiting for transfers between devices, from_root(): return lax.psum(block, axis)  63.9 us
    convert_element_type x8, local copies, waits for them, and re-layouts, one_block(): outer = (outer * inv_seq).astype(jnp.bfloat16)  60 us
    reshape x4, local copies, waits for them, and re-layouts, one_block(): dmixed = douter.reshape(step, cols, width, width).transpose(0, 2, 1, 3).r...  42.6 us
    transpose x4, local copies, waits for them, and re-layouts, one_block(): dmixed = douter.reshape(step, cols, width, width).transpose(0, 2, 1, 3).r...  23.8 us
    all_gather x1, blocking collectives, on_device(): all_seqs = lax.all_gather(packed, 'col', axis=0, tiled=True)  15.8 us
  transfers between devices with their start and end apart: 4, of which 4 were waited for; matrix products, arithmetic and copies ran while one was open for 0% of the time, Pallas kernels for 0%

commit v1 on v0

v1 whole, which is shorter than its diff:
```python
import functools

import jax
import jax.numpy as jnp
from jax import lax
from jax.experimental import pallas as pl
from jax.experimental.pallas import tpu as pltpu
from jax.sharding import PartitionSpec as P

BF16 = jnp.bfloat16
F32 = jnp.float32
MESH = pl.DeviceIdType.MESH
LANES = 128


def nt(x, y):
    return lax.dot_general(x, y, (((1,), (1,)), ((), ())), preferred_element_type=F32)


def nn(x, y):
    return lax.dot_general(x, y, (((1,), (0,)), ((), ())), preferred_element_type=F32)


def tn(x, y):
    return lax.dot_general(x, y, (((0,), (0,)), ((), ())), preferred_element_type=F32)


def iota(shape, dim):
    return lax.broadcasted_iota(jnp.int32, shape, dim)


def one_hot(cond):
    return jnp.where(cond, 1.0, 0.0).astype(BF16)


def wait_bytes(ref, sem):
    pltpu.make_async_copy(ref, ref, sem).wait()


def lane_aligned(start):
    return pl.multiple_of(start, LANES)


def kernel(
    rows,
    cols,
    x_ref,
    gain_ref,
    shift_ref,
    we_ref,
    eshift_ref,
    wf_ref,
    fshift_ref,
    g_hbm,
    pair_hbm,
    align_hbm,
    ow_hbm,
    pw_hbm,
    a_all,
    b_all,
    b_piece,
    gmat,
    wf32,
    w4,
    perm,
    gather_rows,
    scatter_rows,
    aw,
    gp,
    pair_buf,
    align_buf,
    ow_buf,
    pw_buf,
    da_out,
    da_in,
    db_out,
    db_in,
    dw_out,
    dw_in,
    dw_mid,
    dw_fin,
    wg_out,
    wg_in,
    wg_mid,
    wg_fin,
    ready,
    out_sem,
    send,
    recv,
):
    sl, block, feat = x_ref.shape
    width = we_ref.shape[1] // 2
    ch = wf_ref.shape[1]
    ratio = rows // cols
    seqs = sl * cols
    j_len = ratio * block
    inv_seq = 1.0 / seqs
    inv_res = 1.0 / (rows * block)
    me_r = lax.axis_index("row")
    me_c = lax.axis_index("col")

    barrier = pltpu.get_barrier_semaphore()

    def greet_row(k, carry):
        pl.semaphore_signal(
            barrier, inc=1, device_id=(lax.rem(me_r + k, rows), me_c), device_id_type=MESH
        )
        return carry

    def greet_col(k, carry):
        pl.semaphore_signal(
            barrier, inc=1, device_id=(me_r, lax.rem(me_c + k, cols)), device_id_type=MESH
        )
        return carry

    lax.fori_loop(1, rows, greet_row, 0)
    lax.fori_loop(1, cols, greet_col, 0)

    for i in range(block):
        pltpu.make_async_copy(
            g_hbm.at[i], gmat.at[:, pl.ds(i * ch, ch)], out_sem.at[0]
        ).start()

    x = x_ref[...].astype(F32).reshape(sl * block, feat)
    centre = x - jnp.mean(x, axis=-1, keepdims=True)
    inv = lax.rsqrt(jnp.mean(centre * centre, axis=-1, keepdims=True) + 1e-05)
    normed = centre * inv
    gain = gain_ref[...]
    lnout = (normed * gain + shift_ref[...]).astype(BF16)
    we = we_ref[...]
    lane2 = iota((2 * width, 2 * LANES), 1)
    tile_map = one_hot(
        iota((2 * width, 2 * LANES), 0) == (lane2 // LANES) * width + lane2 % width
    )
    we4 = nn(we, tile_map).astype(BF16)
    es = eshift_ref[...]
    es4 = jnp.concatenate([es[:, :width]] * sl + [es[:, width:]] * sl, axis=1)
    proj = nn(lnout, we4) + es4
    owner_lane = (iota((block, 2 * LANES), 1) % LANES) // width
    piece = jnp.zeros((block, 2 * LANES), F32)
    for s in range(sl):
        piece = jnp.where(owner_lane == s, proj[s * block : (s + 1) * block], piece)
    piece = piece.astype(BF16)
    a_all[me_c] = piece[:, :LANES]
    b_piece[...] = piece[:, LANES:]

    pl.semaphore_wait(barrier, rows - 1 + cols - 1)

    def confirm(k, carry):
        pl.semaphore_signal(
            ready, inc=1, device_id=(me_r, lax.rem(me_c + k, cols)), device_id_type=MESH
        )
        return carry

    lax.fori_loop(1, cols, confirm, 0)
    pl.semaphore_wait(ready, cols - 1)

    def to_cols(src, dst, phase):
        def body(k, carry):
            peer = lax.rem(me_c + k, cols)
            pltpu.make_async_remote_copy(
                src_ref=src(peer),
                dst_ref=dst,
                send_sem=send.at[phase],
                recv_sem=recv.at[phase],
                device_id=(me_r, peer),
                device_id_type=MESH,
            ).start()
            return carry

        lax.fori_loop(1, cols, body, 0)

    def to_rows(src, dst, phase):
        def body(k, carry):
            peer = lax.rem(me_r + k, rows)
            pltpu.make_async_remote_copy(
                src_ref=src(peer),
                dst_ref=dst,
                send_sem=send.at[phase],
                recv_sem=recv.at[phase],
                device_id=(peer, me_c),
                device_id_type=MESH,
            ).start()
            return carry

        lax.fori_loop(1, rows, body, 0)

    to_cols(lambda peer: a_all.at[me_c], a_all.at[me_c], 0)
    b_col = me_r // ratio
    b_slot = pl.ds(pl.multiple_of((me_r % ratio) * block, block), block)

    def send_b(k, carry):
        peer = lax.rem(me_r + k, rows)
        own = jnp.logical_and(peer == me_r, b_col == me_c)

        @pl.when(jnp.logical_not(own))
        def _():
            pltpu.make_async_remote_copy(
                src_ref=b_piece,
                dst_ref=b_all.at[me_c, b_slot],
                send_sem=send.at[1],
                recv_sem=recv.at[1],
                device_id=(peer, b_col),
                device_id_type=MESH,
            ).start()

        @pl.when(own)
        def _():
            pltpu.make_async_copy(b_piece, b_all.at[me_c, b_slot], recv.at[1]).start()

        return carry

    lax.fori_loop(0, rows, send_b, 0)

    wf32[...] = wf_ref[...].astype(F32)
    for e in range(width):
        block_e = wf32[pl.ds(e, width, stride=width), :].astype(BF16)
        for s in range(sl):
            w4[s * width : (s + 1) * width, e * ch : (e + 1) * ch] = block_e

    es_len = seqs * width
    step = min(256, es_len)
    for r0 in range(0, es_len, step):
        at_row = iota((step, es_len), 0) + r0
        at_lane = iota((step, es_len), 1)
        perm[r0 : r0 + step, :] = one_hot(
            at_lane == (at_row % seqs) * width + at_row // seqs
        )
    is_len = block * seqs
    qi_len = block * cols
    at_row = iota((is_len, qi_len), 0)
    gather_rows[...] = one_hot(
        iota((is_len, qi_len), 1) == ((at_row % seqs) // sl) * block + at_row // seqs
    )
    at_lane = iota((qi_len, is_len), 1)
    scatter_rows[...] = one_hot(
        iota((qi_len, is_len), 0) == ((at_lane % seqs) // sl) * block + at_lane // seqs
    )
    own_seq = iota((is_len, LANES), 0) % sl == iota((is_len, LANES), 1) // width

    wait_bytes(a_all.at[pl.ds(0, cols - 1)], recv.at[0])
    a_cat = a_all[...].reshape(qi_len, LANES)
    a_rows = (jnp.where(own_seq, nn(gather_rows[...], a_cat), 0.0) * inv_seq).astype(BF16)
    pair_lanes = 2 * ch

    def make_aw(n, carry):
        res = nn(a_rows, w4[:, pl.ds(lane_aligned(n * pair_lanes), pair_lanes)]).astype(BF16)
        for el in range(2):
            at = pl.ds(pl.multiple_of((2 * n + el) * seqs, seqs), seqs)
            for i in range(block):
                aw[at, i * ch : (i + 1) * ch] = res[
                    i * seqs : (i + 1) * seqs, el * ch : (el + 1) * ch
                ]
        return carry

    lax.fori_loop(0, width // 2, make_aw, 0)

    wait_bytes(gmat, out_sem.at[0])
    db_es = jnp.concatenate(
        [nt(gmat[...], aw[n : n + step, :]).astype(BF16) for n in range(0, es_len, step)],
        axis=1,
    )
    db_se = nn(db_es, perm[...]).astype(BF16)
    for q in range(cols):
        db_out[q] = db_se[:, q * LANES : (q + 1) * LANES]

    def send_db(t, carry):
        idx = lax.rem(t + me_r, rows)
        row_to = ratio * me_c + idx // cols
        col_to = idx % cols
        src = db_out.at[col_to, pl.ds(pl.multiple_of((idx // cols) * block, block), block)]
        own = jnp.logical_and(row_to == me_r, col_to == me_c)

        @pl.when(jnp.logical_not(own))
        def _():
            pltpu.make_async_remote_copy(
                src_ref=src,
                dst_ref=db_in.at[me_r],
                send_sem=send.at[3],
                recv_sem=recv.at[3],
                device_id=(row_to, col_to),
                device_id_type=MESH,
            ).start()

        @pl.when(own)
        def _():
            pltpu.make_async_copy(src, db_in.at[me_r], recv.at[3]).start()

        return carry

    lax.fori_loop(0, rows, send_db, 0)

    wait_bytes(b_all, recv.at[1])
    b_cat = jnp.concatenate([b_all[q] for q in range(cols)], axis=1)
    b_t = nt(perm[...], b_cat).astype(BF16)
    b_es = nt(b_cat, perm[...]).astype(BF16)

    def make_g(n, carry):
        res = nn(b_t, gmat[:, pl.ds(lane_aligned(n * pair_lanes), pair_lanes)]).astype(BF16)
        for il in range(2):
            at = pl.ds(pl.multiple_of((2 * n + il) * seqs, seqs), seqs)
            for e in range(width):
                gp[at, e * ch : (e + 1) * ch] = res[
                    e * seqs : (e + 1) * seqs, il * ch : (il + 1) * ch
                ]
        return carry

    lax.fori_loop(0, block // 2, make_g, 0)

    step = min(256, is_len)
    da_rows = jnp.concatenate(
        [nt(gp[n : n + step, :], w4[...]) * inv_seq for n in range(0, is_len, step)], axis=0
    )
    da_rows = jnp.where(own_seq, da_rows, 0.0).astype(BF16)
    da_out[...] = nn(scatter_rows[...], da_rows).astype(BF16).reshape(cols, block, LANES)
    to_cols(lambda peer: da_out.at[peer], da_in.at[me_c], 2)
    da_in[me_c] = da_out[me_c]

    folded = functools.reduce(
        lambda u, v: u + v,
        [a_rows.astype(F32).T[s * width : (s + 1) * width] for s in range(sl)],
    ).astype(BF16)

    def make_dw(n, carry):
        res = nn(folded, gp[:, pl.ds(lane_aligned(n * pair_lanes), pair_lanes)]).astype(BF16)
        for el in range(2):
            dw_out[2 * n + el] = res[:, el * ch : (el + 1) * ch]
        return carry

    lax.fori_loop(0, width // 2, make_dw, 0)
    per_row = width // rows
    to_rows(lambda peer: dw_out.at[pl.ds(peer * per_row, per_row)], dw_in.at[me_r], 4)
    dw_in[me_r] = dw_out[pl.ds(me_r * per_row, per_row)]

    fshift = fshift_ref[...]

    def make_pair(n, carry):
        res = nn(b_es, aw[:, pl.ds(lane_aligned(n * pair_lanes), pair_lanes)])
        for il in range(2):
            pair_buf[2 * n + il] = (res[:, il * ch : (il + 1) * ch] + fshift).astype(BF16)
        at = pl.ds(2 * n, 2)
        pltpu.make_async_copy(pair_buf.at[at], pair_hbm.at[at], out_sem.at[1]).start()
        return carry

    lax.fori_loop(0, block // 2, make_pair, 0)

    wait_bytes(da_in.at[pl.ds(0, cols - 1)], recv.at[2])
    wait_bytes(db_in, recv.at[3])
    da = jnp.sum(da_in[...].astype(F32), axis=0)
    db = jnp.sum(db_in[...].astype(F32), axis=0)
    dproj = jnp.concatenate([da, db], axis=1)
    dproj = jnp.concatenate(
        [jnp.where(owner_lane == s, dproj, 0.0) for s in range(sl)], axis=0
    )
    high = dproj.astype(BF16)
    low = (dproj - high.astype(F32)).astype(BF16)
    wg = tn(high, lnout) + tn(low, lnout)
    wg = jnp.concatenate(
        [
            functools.reduce(
                lambda u, v: u + v,
                [wg[h + s * width : h + (s + 1) * width] for s in range(sl)],
            )
            for h in (0, LANES)
        ],
        axis=0,
    )
    halves = feat // LANES
    part = halves * 2 * width // cols
    wg = jnp.concatenate([wg[:, h * LANES : (h + 1) * LANES] for h in range(halves)], axis=0)
    wg_out[...] = wg.astype(BF16).reshape(cols, part, LANES)
    to_cols(lambda peer: wg_out.at[peer], wg_in.at[me_c], 7)
    wg_in[me_c] = wg_out[me_c]

    wait_bytes(dw_in.at[pl.ds(0, rows - 1)], recv.at[4])
    dw_mid[me_c] = jnp.sum(dw_in[...].astype(F32), axis=0).astype(BF16)
    to_cols(lambda peer: dw_mid.at[me_c], dw_mid.at[me_c], 5)

    dnorm = (nt(high, we4) + nt(low, we4)) * gain
    mean_one = jnp.mean(dnorm, axis=-1, keepdims=True)
    mean_two = jnp.mean(dnorm * normed, axis=-1, keepdims=True)
    align_buf[...] = (inv * (dnorm - mean_one - normed * mean_two)).reshape(sl, block, feat)
    align_copy = pltpu.make_async_copy(align_buf, align_hbm, out_sem.at[2])
    align_copy.start()

    wait_bytes(wg_in.at[pl.ds(0, cols - 1)], recv.at[7])
    wg_mid[me_r] = jnp.sum(wg_in[...].astype(F32), axis=0).astype(BF16)
    to_rows(lambda peer: wg_mid.at[me_r], wg_mid.at[me_r], 8)

    wait_bytes(dw_mid.at[pl.ds(0, cols - 1)], recv.at[5])
    dw_fin[me_r] = (jnp.sum(dw_mid[...].astype(F32), axis=0) * inv_res).astype(BF16)
    to_rows(lambda peer: dw_fin.at[me_r], dw_fin.at[me_r], 6)

    wait_bytes(wg_mid.at[pl.ds(0, rows - 1)], recv.at[8])
    wg_fin[me_c] = (jnp.sum(wg_mid[...].astype(F32), axis=0) * inv_res).astype(BF16)
    to_cols(lambda peer: wg_fin.at[me_c], wg_fin.at[me_c], 9)

    wait_bytes(dw_fin.at[pl.ds(0, rows - 1)], recv.at[6])
    for r in range(rows):
        for k in range(per_row):
            ow_buf[pl.ds(r * per_row + k, width, stride=width), :] = dw_fin[r, k].astype(F32)
    ow_copy = pltpu.make_async_copy(ow_buf, ow_hbm, out_sem.at[3])
    ow_copy.start()

    wait_bytes(wg_fin.at[pl.ds(0, cols - 1)], recv.at[9])
    fin = wg_fin[...].reshape(halves * 2 * width, LANES).astype(F32)
    for h in range(halves):
        pw_buf[h * LANES : (h + 1) * LANES, :] = fin[h * 2 * width : (h + 1) * 2 * width].T
    pw_copy = pltpu.make_async_copy(pw_buf, pw_hbm, out_sem.at[4])
    pw_copy.start()

    wait_bytes(a_all.at[pl.ds(0, cols - 1)], send.at[0])
    for phase in (1, 3):

        @pl.when(b_col == me_c)
        def _():
            wait_bytes(db_in.at[pl.ds(0, rows - 1)], send.at[phase])

        @pl.when(b_col != me_c)
        def _():
            wait_bytes(db_in, send.at[phase])

    wait_bytes(da_in.at[pl.ds(0, cols - 1)], send.at[2])
    wait_bytes(dw_in.at[pl.ds(0, rows - 1)], send.at[4])
    wait_bytes(dw_mid.at[pl.ds(0, cols - 1)], send.at[5])
    wait_bytes(dw_fin.at[pl.ds(0, rows - 1)], send.at[6])
    wait_bytes(wg_in.at[pl.ds(0, cols - 1)], send.at[7])
    wait_bytes(wg_mid.at[pl.ds(0, rows - 1)], send.at[8])
    wait_bytes(wg_fin.at[pl.ds(0, cols - 1)], send.at[9])
    wait_bytes(pair_buf, out_sem.at[1])
    align_copy.wait()
    ow_copy.wait()
    pw_copy.wait()


def on_device(x, gain, shift, we, eshift, wf, fshift, g):
    rows = lax.axis_size("row")
    cols = lax.axis_size("col")
    sl, block, feat = x.shape
    width = we.shape[1] // 2
    ch = wf.shape[1]
    j_len = g.shape[1]
    seqs = sl * cols
    per_row = width // rows
    part = feat * 2 * width // LANES // cols
    vmem = pl.BlockSpec(memory_space=pltpu.VMEM)
    hbm = pl.BlockSpec(memory_space=pl.ANY)

    def buf(*shape, dtype=BF16):
        return pltpu.VMEM(shape, dtype)

    return pl.pallas_call(
        functools.partial(kernel, rows, cols),
        out_shape=[
            jax.ShapeDtypeStruct((block, j_len, ch), BF16),
            jax.ShapeDtypeStruct((sl, block, feat), F32),
            jax.ShapeDtypeStruct((width * width, ch), F32),
            jax.ShapeDtypeStruct((feat, 2 * width), F32),
        ],
        in_specs=[vmem] * 7 + [hbm],
        out_specs=[hbm] * 4,
        scratch_shapes=[
            buf(cols, block, LANES),
            buf(cols, j_len, LANES),
            buf(block, LANES),
            buf(j_len, block * ch),
            buf(width * width, ch, dtype=F32),
            buf(LANES, width * ch),
            buf(seqs * width, seqs * width),
            buf(block * seqs, cols * block),
            buf(cols * block, block * seqs),
            buf(width * seqs, block * ch),
            buf(block * seqs, width * ch),
            buf(block, j_len, ch),
            buf(sl, block, feat, dtype=F32),
            buf(width * width, ch, dtype=F32),
            buf(feat, 2 * width, dtype=F32),
            buf(cols, block, LANES),
            buf(cols, block, LANES),
            buf(cols, j_len, LANES),
            buf(rows, block, LANES),
            buf(width, width, ch),
            buf(rows, per_row, width, ch),
            buf(cols, per_row, width, ch),
            buf(rows, per_row, width, ch),
            buf(cols, part, LANES),
            buf(cols, part, LANES),
            buf(rows, part, LANES),
            buf(cols, part, LANES),
            pltpu.SemaphoreType.REGULAR,
            pltpu.SemaphoreType.DMA((5,)),
            pltpu.SemaphoreType.DMA((10,)),
            pltpu.SemaphoreType.DMA((10,)),
        ],
        compiler_params=pltpu.CompilerParams(
            collective_id=0, has_side_effects=True, vmem_limit_bytes=56 * 1024 * 1024
        ),
        cost_estimate=pl.CostEstimate(
            flops=5_000_000_000, bytes_accessed=4_000_000, transcendentals=0
        ),
    )(
        x,
        gain.reshape(1, -1),
        shift.reshape(1, -1),
        we,
        eshift.reshape(1, -1),
        wf,
        fshift.reshape(1, -1),
        g,
    )


def solution(mesh):
    in_specs = (P("col", "row", None), P(), P(), P(), P(), P(), P(), P("row", "col", None))
    out_specs = (P("row", "col", None), P("col", "row", None), P(), P())
    return jax.shard_map(
        on_device, mesh=mesh, in_specs=in_specs, out_specs=out_specs, check_vma=False
    )
```

time: 776 us -> 82.4 us (0.11)
  waiting for transfers between devices: 533 us -> 0 us
  local copies, waits for them, and re-layouts: 162 us -> 6.94 us
  Pallas kernels: 0 us -> 74.2 us
  matrix products: 33.1 us -> 0 us
  blocking collectives: 15.8 us -> 0 us
  between operations: 14.7 us -> 0.64 us
  other arithmetic: 9.07 us -> 0 us
    psum x3 -> x0, waiting for transfers between devices: 458 us -> none  [the longest x1 255 us: on_device(): lax.psum((weight_gradient, pair_gradient), ('row', 'col'))]
    all_gather x1 -> x0, waiting for transfers between devices: 74.6 us -> none  [on_device(): b_whole = lax.all_gather(b_local, 'row', axis=1, tiled=True)]
    pallas_call x0 -> x1, Pallas kernels: none -> 74.2 us  [on_device(): pl.pallas_call(functools.partial(kernel, rows, cols), out_shape=[jax.Shap...]
    convert_element_type x13 -> x0, local copies, waits for them, and re-layouts: 71.8 us -> none  [the longest x8 60 us: one_block(): outer = (outer * inv_seq).astype(jnp.bfloat16)]
    reshape x8 -> x0, local copies, waits for them, and re-layouts: 43 us -> none  [the longest x4 42.6 us: one_block(): dmixed = douter.reshape(step, cols, width, width).transpose(0, 2, 1, 3).r...]
    dot_general x27 -> x0, matrix products: 33.1 us -> none  [the longest x4 10.8 us: one_block(): lax.dot_general(outer, grad_rows, (((0,), (0,)), ((), ())), preferred_ele...]
    transpose x4 -> x0, local copies, waits for them, and re-layouts: 23.8 us -> none  [one_block(): dmixed = douter.reshape(step, cols, width, width).transpose(0, 2, 1, 3).r...]
    all_gather x1 -> x0, blocking collectives: 15.8 us -> none  [on_device(): all_seqs = lax.all_gather(packed, 'col', axis=0, tiled=True)]
  transfers between devices with their start and end apart: 4 -> 0, of which waited for: 4 -> 0; matrix products, arithmetic and copies ran while one was open for 0% -> 0% of each run, Pallas kernels for 0% -> 0%
where the time goes in v1:
time: 82.4 us; the launch traced here: 81.8 us
  Pallas kernels  74.2 us (90%)
  local copies, waits for them, and re-layouts  6.94 us (8%)
    pallas_call x1, Pallas kernels, on_device(): pl.pallas_call(functools.partial(kernel, rows, cols), out_shape=[jax.Shap...  74.2 us
    unnamed x8, local copies, waits for them, and re-layouts  5.32 us

profile of v1, /device:TPU:1, one launch (start us, length us, event | category | flops | bytes accessed | tf_op | source)
XLA Modules:
  0.0 81.8 jit_solution(14366790445219462213)
XLA Ops:
  0.6 1.5 %copy.12.we_ref = bf16[256,64]{1,0:T(8,128)(2,1)} copy(bf16[256,64]{0,1:T(8,128)(2,1)} %param.11) | data formatting | bytes 65536 | tf_op args[3]
  2.1 74.2 %shard_map.111 = (bf16[32,128,128]{2,1,0:T(8,128)(2,1)}, f32[4,32,256]{2,1,0:T(8,128)}, f32[1024,128]{1,0:T(8,128)}, f32[256,64]{1,0:T(8,128)}) custom-call(bf16[4,32,256]{2,1,0:T(8,128)(2,1)} %x_ref.1, f32[1,256]{1,0:T(1,128)} %bitcast.4, f32[1,256]{1,0:T(1,128)} %bitcast.5, bf16[256,64]{1,0:T(8,128)(2,1)} %copy.12.we_ref, f32[1,64]{1,0:T(1,128)} %bitcast.6, ...), custom_call_target="tpu_custom_call" | custom-call | flops 5000000000 | bytes 4000000 | tf_op jit(solution)/shard_map/pallas_call | solution.py:452
  76.4 1.6 %copy.13 = f32[256,64]{0,1:T(8,128)} copy(f32[256,64]{1,0:T(8,128)} %get-tuple-element.7) | data formatting | bytes 131072 | tf_op jit(solution)/shard_map/pallas_call | solution.py:452
  78.0 0.0 copy-start.1
  78.0 0.0 copy-start
  78.0 2.4 %copy.17 = bf16[32,128,128]{2,1,0:T(8,128)(2,1)} copy(bf16[32,128,128]{2,1,0:T(8,128)(2,1)} %get-tuple-element.12) | data formatting | bytes 2097152
  80.4 0.0 copy-done.1
  80.4 0.7 copy.18
  81.0 0.0 copy-done
  81.0 0.8 copy.19
Async XLA Ops:
  78.0 2.4 %copy-start.1 = (f32[4,32,256]{2,1,0:T(8,128)S(1)}, f32[4,32,256]{2,1,0:T(8,128)}, u32[]{:S(2)}) copy-start(f32[4,32,256]{2,1,0:T(8,128)} %get-tuple-element.13) | copy-start | bytes 393220
  78.0 3.0 %copy-start = (f32[1024,128]{1,0:T(8,128)S(1)}, f32[1024,128]{1,0:T(8,128)}, u32[]{:S(2)}) copy-start(f32[1024,128]{1,0:T(8,128)} %get-tuple-element.14) | copy-start | bytes 1572868

commit v2 on v1

v2 whole, which is shorter than its diff:
```python
import functools

import jax
import jax.numpy as jnp
from jax import lax
from jax.experimental import pallas as pl
from jax.experimental.pallas import tpu as pltpu
from jax.sharding import PartitionSpec as P

BF16 = jnp.bfloat16
F32 = jnp.float32
MESH = pl.DeviceIdType.MESH
LANES = 128


def nt(x, y):
    return lax.dot_general(x, y, (((1,), (1,)), ((), ())), preferred_element_type=F32)


def nn(x, y):
    return lax.dot_general(x, y, (((1,), (0,)), ((), ())), preferred_element_type=F32)


def tn(x, y):
    return lax.dot_general(x, y, (((0,), (0,)), ((), ())), preferred_element_type=F32)


def iota(shape, dim):
    return lax.broadcasted_iota(jnp.int32, shape, dim)


def one_hot(cond):
    return jnp.where(cond, 1.0, 0.0).astype(BF16)


def wait_bytes(ref, sem):
    pltpu.make_async_copy(ref, ref, sem).wait()


def lane_aligned(start):
    return pl.multiple_of(start, LANES)


def kernel(
    rows,
    cols,
    x_hbm,
    we_hbm,
    gain_hbm,
    shift_hbm,
    eshift_hbm,
    fshift_hbm,
    wf_hbm,
    g_hbm,
    pair_hbm,
    align_hbm,
    ow_hbm,
    pw_hbm,
    x_ref,
    we_ref,
    gain_ref,
    shift_ref,
    eshift_ref,
    fshift_ref,
    wf_ref,
    a_all,
    b_all,
    b_piece,
    b_relay,
    gmat,
    wf32,
    w4,
    perm,
    gather_rows,
    scatter_rows,
    aw,
    gp,
    pair_buf,
    align_buf,
    ow_buf,
    pw_buf,
    da_out,
    da_in,
    db_out,
    db_in,
    dw_out,
    dw_in,
    dw_mid,
    dw_fin,
    wg_out,
    wg_in,
    wg_mid,
    wg_fin,
    ready,
    in_sem,
    out_sem,
    send,
    recv,
):
    sl, block, feat = x_ref.shape
    width = we_ref.shape[0] // 2
    ch = wf_ref.shape[1]
    ratio = rows // cols
    seqs = sl * cols
    j_len = ratio * block
    inv_seq = 1.0 / seqs
    inv_res = 1.0 / (rows * block)
    me_r = lax.axis_index("row")
    me_c = lax.axis_index("col")
    near = cols // 2
    nz = rows // near
    y, z = me_r // nz, lax.rem(me_r, nz)
    x, core = me_c // 2, lax.rem(me_c, 2)
    group = near * cols
    member = y * cols + me_c

    def in_group(m):
        return ((m // cols) * nz + z, lax.rem(m, cols))

    def in_z(k):
        return (y * nz + k, me_c)

    barrier = pltpu.get_barrier_semaphore()

    def greet_group(k, carry):
        pl.semaphore_signal(
            barrier,
            inc=1,
            device_id=in_group(lax.rem(member + k, group)),
            device_id_type=MESH,
        )
        return carry

    def greet_z(k, carry):
        pl.semaphore_signal(
            barrier, inc=1, device_id=in_z(lax.rem(z + k, nz)), device_id_type=MESH
        )
        return carry

    loads = [
        pltpu.make_async_copy(src, dst, in_sem.at[k])
        for k, (src, dst) in enumerate(
            (
                (x_hbm, x_ref),
                (we_hbm, we_ref),
                (gain_hbm, gain_ref),
                (shift_hbm, shift_ref),
                (eshift_hbm, eshift_ref),
                (fshift_hbm, fshift_ref),
                (wf_hbm, wf_ref),
            )
        )
    ]
    for load in loads:
        load.start()
    lax.fori_loop(1, group, greet_group, 0)
    lax.fori_loop(1, nz, greet_z, 0)

    for i in range(block):
        pltpu.make_async_copy(
            g_hbm.at[i], gmat.at[:, pl.ds(i * ch, ch)], out_sem.at[0]
        ).start()

    loads[0].wait()
    xf = x_ref[...].astype(F32).reshape(sl * block, feat)
    centre = xf - jnp.mean(xf, axis=-1, keepdims=True)
    inv = lax.rsqrt(jnp.mean(centre * centre, axis=-1, keepdims=True) + 1e-05)
    normed = centre * inv
    for load in loads[1:-1]:
        load.wait()
    gain = gain_ref[...]
    lnout = (normed * gain + shift_ref[...]).astype(BF16)
    we = we_ref[...]
    we4 = jnp.concatenate([we[:width]] * sl + [we[width:]] * sl, axis=0)
    es = eshift_ref[...]
    es4 = jnp.concatenate([es[:, :width]] * sl + [es[:, width:]] * sl, axis=1)
    fshift = fshift_ref[...]
    proj = nt(lnout, we4) + es4
    owner_lane = (iota((block, 2 * LANES), 1) % LANES) // width
    piece = jnp.zeros((block, 2 * LANES), F32)
    for s in range(sl):
        piece = jnp.where(owner_lane == s, proj[s * block : (s + 1) * block], piece)
    piece = piece.astype(BF16)
    a_all[me_c] = piece[:, :LANES]
    b_piece[...] = piece[:, LANES:]

    pl.semaphore_wait(barrier, group - 1 + nz - 1)

    def send_all(count, peer_of, device_of, src, dst, phase):
        def body(k, carry):
            peer = peer_of(k)
            pltpu.make_async_remote_copy(
                src_ref=src(peer),
                dst_ref=dst,
                send_sem=send.at[phase],
                recv_sem=recv.at[phase],
                device_id=device_of(peer),
                device_id_type=MESH,
            ).start()
            return carry

        lax.fori_loop(1, count, body, 0)

    def to_cols(src, dst, phase):
        send_all(
            cols, lambda k: lax.rem(me_c + k, cols), lambda p: (me_r, p), src, dst, phase
        )

    def to_group(src, dst, phase):
        send_all(group, lambda k: lax.rem(member + k, group), in_group, src, dst, phase)

    def to_z(src, dst, phase):
        send_all(nz, lambda k: lax.rem(z + k, nz), in_z, src, dst, phase)

    to_cols(lambda peer: a_all.at[me_c], a_all.at[me_c], 0)
    relay = pltpu.make_async_remote_copy(
        src_ref=b_piece,
        dst_ref=b_relay,
        send_sem=send.at[1],
        recv_sem=recv.at[1],
        device_id=(x * nz + z, y * 2 + core),
        device_id_type=MESH,
    )

    @pl.when(x != y)
    def _():
        relay.start()

    @pl.when(x == y)
    def _():
        pltpu.make_async_copy(b_piece, b_relay, recv.at[1]).start()

    def confirm(k, carry):
        pl.semaphore_signal(
            ready,
            inc=1,
            device_id=in_group(lax.rem(member + k, group)),
            device_id_type=MESH,
        )
        return carry

    lax.fori_loop(1, group, confirm, 0)

    loads[-1].wait()
    wf32[...] = wf_ref[...].astype(F32)
    for e in range(width):
        block_e = wf32[pl.ds(e, width, stride=width), :].astype(BF16)
        for s in range(sl):
            w4[s * width : (s + 1) * width, e * ch : (e + 1) * ch] = block_e

    es_len = seqs * width
    step = min(256, es_len)
    for r0 in range(0, es_len, step):
        at_row = iota((step, es_len), 0) + r0
        at_lane = iota((step, es_len), 1)
        perm[r0 : r0 + step, :] = one_hot(
            at_lane == (at_row % seqs) * width + at_row // seqs
        )
    is_len = block * seqs
    qi_len = block * cols
    at_row = iota((is_len, qi_len), 0)
    gather_rows[...] = one_hot(
        iota((is_len, qi_len), 1) == ((at_row % seqs) // sl) * block + at_row // seqs
    )
    at_lane = iota((qi_len, is_len), 1)
    scatter_rows[...] = one_hot(
        iota((qi_len, is_len), 0) == ((at_lane % seqs) // sl) * block + at_lane // seqs
    )
    own_seq = iota((is_len, LANES), 0) % sl == iota((is_len, LANES), 1) // width

    pl.semaphore_wait(ready, group - 1)
    wait_bytes(b_relay, recv.at[1])
    b_col = x * 2 + z // ratio
    b_slot = pl.ds(pl.multiple_of(lax.rem(z, ratio) * block, block), block)
    b_from = y * 2 + core

    def send_b(k, carry):
        peer = lax.rem(me_r + k, rows)
        own = jnp.logical_and(peer == me_r, b_col == me_c)

        @pl.when(jnp.logical_not(own))
        def _():
            pltpu.make_async_remote_copy(
                src_ref=b_relay,
                dst_ref=b_all.at[b_from, b_slot],
                send_sem=send.at[2],
                recv_sem=recv.at[2],
                device_id=(peer, b_col),
                device_id_type=MESH,
            ).start()

        @pl.when(own)
        def _():
            pltpu.make_async_copy(b_relay, b_all.at[b_from, b_slot], recv.at[2]).start()

        return carry

    lax.fori_loop(0, rows, send_b, 0)

    wait_bytes(a_all.at[pl.ds(0, cols - 1)], recv.at[0])
    a_cat = a_all[...].reshape(qi_len, LANES)
    a_rows = (jnp.where(own_seq, nn(gather_rows[...], a_cat), 0.0) * inv_seq).astype(BF16)
    pair_lanes = 2 * ch

    def make_aw(n, carry):
        res = nn(a_rows, w4[:, pl.ds(lane_aligned(n * pair_lanes), pair_lanes)]).astype(BF16)
        for el in range(2):
            at = pl.ds(pl.multiple_of((2 * n + el) * seqs, seqs), seqs)
            for i in range(block):
                aw[at, i * ch : (i + 1) * ch] = res[
                    i * seqs : (i + 1) * seqs, el * ch : (el + 1) * ch
                ]
        return carry

    lax.fori_loop(0, width // 2, make_aw, 0)

    wait_bytes(gmat, out_sem.at[0])
    db_es = jnp.concatenate(
        [nt(gmat[...], aw[n : n + step, :]).astype(BF16) for n in range(0, es_len, step)],
        axis=1,
    )
    db_se = nn(db_es, perm[...]).astype(BF16)
    for q in range(cols):
        db_out[q] = db_se[:, q * LANES : (q + 1) * LANES]

    def send_db(t, carry):
        idx = lax.rem(t + me_r, rows)
        row_to = ratio * me_c + idx // cols
        col_to = idx % cols
        src = db_out.at[col_to, pl.ds(pl.multiple_of((idx // cols) * block, block), block)]
        own = jnp.logical_and(row_to == me_r, col_to == me_c)

        @pl.when(jnp.logical_not(own))
        def _():
            pltpu.make_async_remote_copy(
                src_ref=src,
                dst_ref=db_in.at[me_r],
                send_sem=send.at[3],
                recv_sem=recv.at[3],
                device_id=(row_to, col_to),
                device_id_type=MESH,
            ).start()

        @pl.when(own)
        def _():
            pltpu.make_async_copy(src, db_in.at[me_r], recv.at[3]).start()

        return carry

    lax.fori_loop(0, rows, send_db, 0)

    wait_bytes(b_all, recv.at[2])
    b_cat = jnp.concatenate([b_all[q] for q in range(cols)], axis=1)
    b_t = nt(perm[...], b_cat).astype(BF16)
    b_es = nt(b_cat, perm[...]).astype(BF16)

    def make_g(n, carry):
        res = nn(b_t, gmat[:, pl.ds(lane_aligned(n * pair_lanes), pair_lanes)]).astype(BF16)
        for il in range(2):
            at = pl.ds(pl.multiple_of((2 * n + il) * seqs, seqs), seqs)
            for e in range(width):
                gp[at, e * ch : (e + 1) * ch] = res[
                    e * seqs : (e + 1) * seqs, il * ch : (il + 1) * ch
                ]
        return carry

    lax.fori_loop(0, block // 2, make_g, 0)

    folded = functools.reduce(
        lambda u, v: u + v,
        [a_rows.astype(F32).T[s * width : (s + 1) * width] for s in range(sl)],
    ).astype(BF16)

    def make_dw(n, carry):
        res = nn(folded, gp[:, pl.ds(lane_aligned(n * pair_lanes), pair_lanes)]).astype(BF16)
        for el in range(2):
            dw_out[2 * n + el] = res[:, el * ch : (el + 1) * ch]
        return carry

    lax.fori_loop(0, width // 2, make_dw, 0)
    share = width // group
    to_group(lambda peer: dw_out.at[pl.ds(peer * share, share)], dw_in.at[member], 5)
    dw_in[member] = dw_out[pl.ds(member * share, share)]

    step = min(256, is_len)
    da_rows = jnp.concatenate(
        [nt(gp[n : n + step, :], w4[...]) * inv_seq for n in range(0, is_len, step)], axis=0
    )
    da_rows = jnp.where(own_seq, da_rows, 0.0).astype(BF16)
    da_out[...] = nn(scatter_rows[...], da_rows).astype(BF16).reshape(cols, block, LANES)
    to_cols(lambda peer: da_out.at[peer], da_in.at[me_c], 4)
    da_in[me_c] = da_out[me_c]

    def make_pair(n, carry):
        res = nn(b_es, aw[:, pl.ds(lane_aligned(n * pair_lanes), pair_lanes)])
        for il in range(2):
            pair_buf[2 * n + il] = (res[:, il * ch : (il + 1) * ch] + fshift).astype(BF16)
        at = pl.ds(2 * n, 2)
        pltpu.make_async_copy(pair_buf.at[at], pair_hbm.at[at], out_sem.at[1]).start()
        return carry

    lax.fori_loop(0, block // 4, make_pair, 0)

    wait_bytes(da_in.at[pl.ds(0, cols - 1)], recv.at[4])
    wait_bytes(db_in, recv.at[3])
    da = jnp.sum(da_in[...].astype(F32), axis=0)
    db = jnp.sum(db_in[...].astype(F32), axis=0)
    dproj = jnp.concatenate([da, db], axis=1)
    dproj = jnp.concatenate(
        [jnp.where(owner_lane == s, dproj, 0.0) for s in range(sl)], axis=0
    )
    high = dproj.astype(BF16)
    low = (dproj - high.astype(F32)).astype(BF16)
    wg = tn(high, lnout) + tn(low, lnout)
    wg = jnp.concatenate(
        [
            functools.reduce(
                lambda u, v: u + v,
                [wg[h + s * width : h + (s + 1) * width] for s in range(sl)],
            )
            for h in (0, LANES)
        ],
        axis=0,
    )
    halves = feat // LANES
    part = halves * 2 * width // group
    for h in range(halves):
        for k in range(2 * width // part):
            wg_out[h * 2 * width // part + k] = wg[
                k * part : (k + 1) * part, h * LANES : (h + 1) * LANES
            ]
    to_group(lambda peer: wg_out.at[peer], wg_in.at[member], 8)
    wg_in[member] = wg_out[member]

    lax.fori_loop(block // 4, block // 2, make_pair, 0)

    wait_bytes(dw_in.at[pl.ds(0, group - 1)], recv.at[5])
    dw_mid[z] = jnp.sum(dw_in[...].astype(F32), axis=0).astype(BF16)
    to_z(lambda peer: dw_mid.at[z], dw_mid.at[z], 6)

    dnorm = (nn(high, we4) + nn(low, we4)) * gain
    mean_one = jnp.mean(dnorm, axis=-1, keepdims=True)
    mean_two = jnp.mean(dnorm * normed, axis=-1, keepdims=True)
    align_buf[...] = (inv * (dnorm - mean_one - normed * mean_two)).reshape(sl, block, feat)
    align_copy = pltpu.make_async_copy(align_buf, align_hbm, out_sem.at[2])
    align_copy.start()

    wait_bytes(wg_in.at[pl.ds(0, group - 1)], recv.at[8])
    wg_mid[z] = jnp.sum(wg_in[...], axis=0)
    to_z(lambda peer: wg_mid.at[z], wg_mid.at[z], 9)

    wait_bytes(dw_mid.at[pl.ds(0, nz - 1)], recv.at[6])
    dw_fin[member] = (jnp.sum(dw_mid[...].astype(F32), axis=0) * inv_res).astype(BF16)
    to_group(lambda peer: dw_fin.at[member], dw_fin.at[member], 7)

    wait_bytes(wg_mid.at[pl.ds(0, nz - 1)], recv.at[9])
    wg_fin[member] = jnp.sum(wg_mid[...], axis=0) * inv_res
    to_group(lambda peer: wg_fin.at[member], wg_fin.at[member], 10)

    wait_bytes(dw_fin.at[pl.ds(0, group - 1)], recv.at[7])
    for m in range(group):
        for k in range(share):
            ow_buf[pl.ds(m * share + k, width, stride=width), :] = dw_fin[m, k].astype(F32)
    ow_copy = pltpu.make_async_copy(ow_buf, ow_hbm, out_sem.at[3])
    ow_copy.start()

    wait_bytes(wg_fin.at[pl.ds(0, group - 1)], recv.at[10])
    for h in range(halves):
        for k in range(2 * width // part):
            pw_buf[k * part : (k + 1) * part, h * LANES : (h + 1) * LANES] = wg_fin[
                h * 2 * width // part + k
            ]
    pw_copy = pltpu.make_async_copy(pw_buf, pw_hbm, out_sem.at[4])
    pw_copy.start()

    wait_bytes(a_all.at[pl.ds(0, cols - 1)], send.at[0])

    @pl.when(x != y)
    def _():
        relay.wait_send()

    @pl.when(b_col == me_c)
    def _():
        wait_bytes(db_in.at[pl.ds(0, rows - 1)], send.at[2])

    @pl.when(b_col != me_c)
    def _():
        wait_bytes(db_in, send.at[2])

    @pl.when(me_r // ratio == me_c)
    def _():
        wait_bytes(db_in.at[pl.ds(0, rows - 1)], send.at[3])

    @pl.when(me_r // ratio != me_c)
    def _():
        wait_bytes(db_in, send.at[3])

    wait_bytes(da_in.at[pl.ds(0, cols - 1)], send.at[4])
    wait_bytes(dw_in.at[pl.ds(0, group - 1)], send.at[5])
    wait_bytes(dw_mid.at[pl.ds(0, nz - 1)], send.at[6])
    wait_bytes(dw_fin.at[pl.ds(0, group - 1)], send.at[7])
    wait_bytes(wg_in.at[pl.ds(0, group - 1)], send.at[8])
    wait_bytes(wg_mid.at[pl.ds(0, nz - 1)], send.at[9])
    wait_bytes(wg_fin.at[pl.ds(0, group - 1)], send.at[10])
    wait_bytes(pair_buf, out_sem.at[1])
    align_copy.wait()
    ow_copy.wait()
    pw_copy.wait()


def copy_kernel(*refs):
    sem = refs[-1]
    parts = []
    for src, held, dst in zip(refs[0:4], refs[8:12], refs[4:8]):
        count = 4 if src.shape[0] * src.shape[1] >= 1024 else 1
        rows = src.shape[0] // count
        for k in range(count):
            at = pl.ds(k * rows, rows)
            n = len(parts)
            parts.append(
                (
                    pltpu.make_async_copy(src.at[at], held.at[at], sem.at[0, n]),
                    pltpu.make_async_copy(held.at[at], dst.at[at], sem.at[1, n]),
                )
            )
    for load, _ in parts:
        load.start()
    for load, store in parts:
        load.wait()
        store.start()
    for _, store in parts:
        store.wait()


def on_device(x, gain, shift, we, eshift, wf, fshift, g):
    rows = lax.axis_size("row")
    cols = lax.axis_size("col")
    sl, block, feat = x.shape
    width = we.shape[1] // 2
    ch = wf.shape[1]
    j_len = g.shape[1]
    seqs = sl * cols
    near = cols // 2
    nz = rows // near
    group = near * cols
    share = width // group
    part = feat * 2 * width // LANES // group
    hbm = pl.BlockSpec(memory_space=pl.ANY)

    def buf(*shape, dtype=BF16):
        return pltpu.VMEM(shape, dtype)

    shapes = [
        jax.ShapeDtypeStruct((block, j_len, ch), BF16),
        jax.ShapeDtypeStruct((sl, block, feat), F32),
        jax.ShapeDtypeStruct((width * width, ch), F32),
        jax.ShapeDtypeStruct((2 * width, feat), F32),
    ]
    outs = pl.pallas_call(
        functools.partial(kernel, rows, cols),
        out_shape=shapes,
        in_specs=[hbm] * 8,
        out_specs=[hbm] * 4,
        scratch_shapes=[
            buf(sl, block, feat),
            buf(2 * width, feat),
            buf(1, feat, dtype=F32),
            buf(1, feat, dtype=F32),
            buf(1, 2 * width, dtype=F32),
            buf(1, ch, dtype=F32),
            buf(width * width, ch),
            buf(cols, block, LANES),
            buf(cols, j_len, LANES),
            buf(block, LANES),
            buf(block, LANES),
            buf(j_len, block * ch),
            buf(width * width, ch, dtype=F32),
            buf(LANES, width * ch),
            buf(seqs * width, seqs * width),
            buf(block * seqs, cols * block),
            buf(cols * block, block * seqs),
            buf(width * seqs, block * ch),
            buf(block * seqs, width * ch),
            buf(block, j_len, ch),
            buf(sl, block, feat, dtype=F32),
            buf(width * width, ch, dtype=F32),
            buf(2 * width, feat, dtype=F32),
            buf(cols, block, LANES),
            buf(cols, block, LANES),
            buf(cols, j_len, LANES),
            buf(rows, block, LANES),
            buf(width, width, ch),
            buf(group, share, width, ch),
            buf(nz, share, width, ch),
            buf(group, share, width, ch),
            buf(group, part, LANES, dtype=F32),
            buf(group, part, LANES, dtype=F32),
            buf(nz, part, LANES, dtype=F32),
            buf(group, part, LANES, dtype=F32),
            pltpu.SemaphoreType.REGULAR,
            pltpu.SemaphoreType.DMA((7,)),
            pltpu.SemaphoreType.DMA((5,)),
            pltpu.SemaphoreType.DMA((11,)),
            pltpu.SemaphoreType.DMA((11,)),
        ],
        compiler_params=pltpu.CompilerParams(
            collective_id=0, has_side_effects=True, vmem_limit_bytes=56 * 1024 * 1024
        ),
        cost_estimate=pl.CostEstimate(
            flops=5_000_000_000, bytes_accessed=4_000_000, transcendentals=0
        ),
    )(
        x,
        we.T,
        gain.reshape(1, feat),
        shift.reshape(1, feat),
        eshift.reshape(1, 2 * width),
        fshift.reshape(1, ch),
        wf,
        g,
    )
    pair, align, ow, pw = pl.pallas_call(
        copy_kernel,
        out_shape=shapes,
        in_specs=[hbm] * 4,
        out_specs=[hbm] * 4,
        scratch_shapes=[pltpu.VMEM(v.shape, v.dtype) for v in shapes]
        + [pltpu.SemaphoreType.DMA((2, 16))],
        compiler_params=pltpu.CompilerParams(vmem_limit_bytes=56 * 1024 * 1024),
    )(*outs)
    return pair, align, ow, pw.T


def solution(mesh):
    in_specs = (P("col", "row", None), P(), P(), P(), P(), P(), P(), P("row", "col", None))
    out_specs = (P("row", "col", None), P("col", "row", None), P(), P())
    return jax.shard_map(
        on_device, mesh=mesh, in_specs=in_specs, out_specs=out_specs, check_vma=False
    )
```

time: 82.4 us -> 61 us (0.74)
  Pallas kernels: 74.2 us -> 60.3 us
  local copies, waits for them, and re-layouts: 6.94 us -> 0 us
    pallas_call x1 -> x2, Pallas kernels: 74.2 us -> 60.3 us  [the longest x1 57.9 us: on_device(): pl.pallas_call(functools.partial(kernel, rows, cols), out_shape=shapes, i...]
    unnamed x8 -> x0, local copies, waits for them, and re-layouts: 5.32 us -> none
    pallas_call x1 -> x0, local copies, waits for them, and re-layouts: 1.62 us -> none  [on_device(): pl.pallas_call(functools.partial(kernel, rows, cols), out_shape=[jax.Shap...]
where the time goes in v2:
time: 61 us; the launch traced here: 60.9 us
  Pallas kernels  60.3 us (99%)
  between operations  0.64 us (1%)
    pallas_call x1, Pallas kernels, on_device(): pl.pallas_call(functools.partial(kernel, rows, cols), out_shape=shapes, i...  57.9 us
    pallas_call x1, Pallas kernels, on_device(): pl.pallas_call(copy_kernel, out_shape=shapes, in_specs=[hbm] * 4, out_spe...  2.41 us

profile of v2, /device:TPU:1, one launch (start us, length us, event | category | flops | bytes accessed | tf_op | source)
XLA Modules:
  0.0 60.9 jit_solution(15085196090066676317)
XLA Ops:
  0.6 57.9 %shard_map.111 = (bf16[32,128,128]{2,1,0:T(8,128)(2,1)}, f32[4,32,256]{2,1,0:T(8,128)}, f32[1024,128]{1,0:T(8,128)}, f32[64,256]{1,0:T(8,128)}) custom-call(bf16[4,32,256]{2,1,0:T(8,128)(2,1)} %x_hbm.1, bf16[64,256]{1,0:T(8,128)(2,1)} %bitcast.7, f32[1,256]{1,0:T(1,128)} %bitcast.8, f32[1,256]{1,0:T(1,128)} %bitcast.9, f32[1,64]{1,0:T(1,128)} %bitcast.10, ...), custom_call_target="tpu_custom_call" | custom-call | flops 5000000000 | bytes 4000000 | tf_op jit(solution)/shard_map/pallas_call | solution.py:559
  58.5 2.4 %shard_map.112 = (bf16[32,128,128]{2,1,0:T(8,128)(2,1)}, f32[4,32,256]{2,1,0:T(8,128)}, f32[1024,128]{1,0:T(8,128)}, f32[64,256]{1,0:T(8,128)}) custom-call(bf16[32,128,128]{2,1,0:T(8,128)(2,1)} %get-tuple-element.12.refs_0_, f32[4,32,256]{2,1,0:T(8,128)} %get-tuple-element.13.refs_1_, f32[1024,128]{1,0:T(8,128)} %get-tuple-element.14.refs_2_, ...), custom_call_target="tpu_custom_call" | custom-call | tf_op jit(solution)/shard_map/pallas_call | solution.py:622

commit v3 on v2

--- a/solution.py
+++ b/solution.py
@@ -70,7 +70,9 @@
     gmat,
     wf32,
     w4,
-    perm,
+    a_rows_ref,
+    held,
+    b_t,
     gather_rows,
     scatter_rows,
     aw,
@@ -249,13 +251,6 @@
             w4[s * width : (s + 1) * width, e * ch : (e + 1) * ch] = block_e
 
     es_len = seqs * width
-    step = min(256, es_len)
-    for r0 in range(0, es_len, step):
-        at_row = iota((step, es_len), 0) + r0
-        at_lane = iota((step, es_len), 1)
-        perm[r0 : r0 + step, :] = one_hot(
-            at_lane == (at_row % seqs) * width + at_row // seqs
-        )
     is_len = block * seqs
     qi_len = block * cols
     at_row = iota((is_len, qi_len), 0)
@@ -299,29 +294,35 @@
 
     wait_bytes(a_all.at[pl.ds(0, cols - 1)], recv.at[0])
     a_cat = a_all[...].reshape(qi_len, LANES)
-    a_rows = (jnp.where(own_seq, nn(gather_rows[...], a_cat), 0.0) * inv_seq).astype(BF16)
-    pair_lanes = 2 * ch
-
-    def make_aw(n, carry):
-        res = nn(a_rows, w4[:, pl.ds(lane_aligned(n * pair_lanes), pair_lanes)]).astype(BF16)
-        for el in range(2):
-            at = pl.ds(pl.multiple_of((2 * n + el) * seqs, seqs), seqs)
-            for i in range(block):
-                aw[at, i * ch : (i + 1) * ch] = res[
-                    i * seqs : (i + 1) * seqs, el * ch : (el + 1) * ch
-                ]
+    a_rows_ref[...] = (jnp.where(own_seq, nn(gather_rows[...], a_cat), 0.0) * inv_seq).astype(
+        BF16
+    )
+    chunk = min(256, is_len)
+    lanes = 4 * ch
+
+    def make_aw(m, carry):
+        lhs = a_rows_ref[pl.ds(pl.multiple_of(m * chunk, chunk), chunk), :]
+        per = chunk // seqs
+        for n in range(width // 4):
+            res = nn(lhs, w4[:, n * lanes : (n + 1) * lanes]).astype(BF16)
+            for el in range(4):
+                e = 4 * n + el
+                for il in range(per):
+                    at = pl.ds(lane_aligned((m * per + il) * ch), ch)
+                    aw[e * seqs : (e + 1) * seqs, at] = res[
+                        il * seqs : (il + 1) * seqs, el * ch : (el + 1) * ch
+                    ]
         return carry
 
-    lax.fori_loop(0, width // 2, make_aw, 0)
+    lax.fori_loop(0, is_len // chunk, make_aw, 0, unroll=2)
 
     wait_bytes(gmat, out_sem.at[0])
-    db_es = jnp.concatenate(
-        [nt(gmat[...], aw[n : n + step, :]).astype(BF16) for n in range(0, es_len, step)],
-        axis=1,
-    )
-    db_se = nn(db_es, perm[...]).astype(BF16)
+    step = min(512, es_len)
+    for n in range(0, es_len, step):
+        held[n : n + step, :] = nt(aw[n : n + step, :], gmat[...])
     for q in range(cols):
-        db_out[q] = db_se[:, q * LANES : (q + 1) * LANES]
+        rows_q = [held[pl.ds(q * sl + s, width, stride=seqs), :] for s in range(sl)]
+        db_out[q] = jnp.concatenate(rows_q, axis=0).T.astype(BF16)
 
     def send_db(t, carry):
         idx = lax.rem(t + me_r, rows)
@@ -350,39 +351,40 @@
     lax.fori_loop(0, rows, send_db, 0)
 
     wait_bytes(b_all, recv.at[2])
-    b_cat = jnp.concatenate([b_all[q] for q in range(cols)], axis=1)
-    b_t = nt(perm[...], b_cat).astype(BF16)
-    b_es = nt(b_cat, perm[...]).astype(BF16)
-
-    def make_g(n, carry):
-        res = nn(b_t, gmat[:, pl.ds(lane_aligned(n * pair_lanes), pair_lanes)]).astype(BF16)
-        for il in range(2):
-            at = pl.ds(pl.multiple_of((2 * n + il) * seqs, seqs), seqs)
-            for e in range(width):
-                gp[at, e * ch : (e + 1) * ch] = res[
-                    e * seqs : (e + 1) * seqs, il * ch : (il + 1) * ch
-                ]
+    for q in range(cols):
+        held[q * LANES : (q + 1) * LANES, :] = b_all[q].astype(F32).T
+    for e in range(width):
+        b_t[e * seqs : (e + 1) * seqs, :] = held[pl.ds(e, seqs, stride=width), :].astype(BF16)
+
+    def make_g(m, carry):
+        lhs = b_t[pl.ds(pl.multiple_of(m * chunk, chunk), chunk), :]
+        per = chunk // seqs
+        for n in range(block // 4):
+            res = nn(lhs, gmat[:, n * lanes : (n + 1) * lanes]).astype(BF16)
+            for il in range(4):
+                i = 4 * n + il
+                for el in range(per):
+                    at = pl.ds(lane_aligned((m * per + el) * ch), ch)
+                    gp[i * seqs : (i + 1) * seqs, at] = res[
+                        el * seqs : (el + 1) * seqs, il * ch : (il + 1) * ch
+                    ]
         return carry
 
-    lax.fori_loop(0, block // 2, make_g, 0)
-
-    folded = functools.reduce(
-        lambda u, v: u + v,
-        [a_rows.astype(F32).T[s * width : (s + 1) * width] for s in range(sl)],
-    ).astype(BF16)
-
-    def make_dw(n, carry):
-        res = nn(folded, gp[:, pl.ds(lane_aligned(n * pair_lanes), pair_lanes)]).astype(BF16)
-        for el in range(2):
-            dw_out[2 * n + el] = res[:, el * ch : (el + 1) * ch]
-        return carry
-
-    lax.fori_loop(0, width // 2, make_dw, 0)
+    lax.fori_loop(0, es_len // chunk, make_g, 0, unroll=2)
+
+    half = width // 2
+    for h in range(2):
+        res = tn(a_rows_ref[...], gp[:, h * half * ch : (h + 1) * half * ch])
+        res = functools.reduce(
+            lambda u, v: u + v, [res[s * width : (s + 1) * width] for s in range(sl)]
+        ).astype(BF16)
+        for el in range(half):
+            dw_out[h * half + el] = res[:, el * ch : (el + 1) * ch]
     share = width // group
     to_group(lambda peer: dw_out.at[pl.ds(peer * share, share)], dw_in.at[member], 5)
     dw_in[member] = dw_out[pl.ds(member * share, share)]
 
-    step = min(256, is_len)
+    step = min(512, is_len)
     da_rows = jnp.concatenate(
         [nt(gp[n : n + step, :], w4[...]) * inv_seq for n in range(0, is_len, step)], axis=0
     )
@@ -391,15 +393,16 @@
     to_cols(lambda peer: da_out.at[peer], da_in.at[me_c], 4)
     da_in[me_c] = da_out[me_c]
 
-    def make_pair(n, carry):
-        res = nn(b_es, aw[:, pl.ds(lane_aligned(n * pair_lanes), pair_lanes)])
-        for il in range(2):
-            pair_buf[2 * n + il] = (res[:, il * ch : (il + 1) * ch] + fshift).astype(BF16)
-        at = pl.ds(2 * n, 2)
+    b_es = jnp.concatenate(
+        [b_t[n : n + LANES, :].T for n in range(0, es_len, LANES)], axis=1
+    )
+    half = block // 2
+    for h in range(2):
+        res = nn(b_es, aw[:, h * half * ch : (h + 1) * half * ch])
+        for il in range(half):
+            pair_buf[h * half + il] = (res[:, il * ch : (il + 1) * ch] + fshift).astype(BF16)
+        at = pl.ds(h * half, half)
         pltpu.make_async_copy(pair_buf.at[at], pair_hbm.at[at], out_sem.at[1]).start()
-        return carry
-
-    lax.fori_loop(0, block // 4, make_pair, 0)
 
     wait_bytes(da_in.at[pl.ds(0, cols - 1)], recv.at[4])
     wait_bytes(db_in, recv.at[3])
@@ -431,8 +434,6 @@
             ]
     to_group(lambda peer: wg_out.at[peer], wg_in.at[member], 8)
     wg_in[member] = wg_out[member]
-
-    lax.fori_loop(block // 4, block // 2, make_pair, 0)
 
     wait_bytes(dw_in.at[pl.ds(0, group - 1)], recv.at[5])
     dw_mid[z] = jnp.sum(dw_in[...].astype(F32), axis=0).astype(BF16)
@@ -576,7 +577,9 @@
             buf(j_len, block * ch),
             buf(width * width, ch, dtype=F32),
             buf(LANES, width * ch),
-            buf(seqs * width, seqs * width),
+            buf(block * seqs, LANES),
+            buf(seqs * width, j_len, dtype=F32),
+            buf(seqs * width, j_len),
             buf(block * seqs, cols * block),
             buf(cols * block, block * seqs),
             buf(width * seqs, block * ch),

time: 61 us -> 54 us (0.89)
  Pallas kernels: 60.3 us -> 53.3 us
    pallas_call x1, Pallas kernels: 57.9 us -> 50.9 us  [on_device(): pl.pallas_call(functools.partial(kernel, rows, cols), out_shape=shapes, i...]
where the time goes in v3:
time: 54 us; the launch traced here: 53.9 us
  Pallas kernels  53.3 us (99%)
  between operations  0.64 us (1%)
    pallas_call x1, Pallas kernels, on_device(): pl.pallas_call(functools.partial(kernel, rows, cols), out_shape=shapes, i...  50.9 us
    pallas_call x1, Pallas kernels, on_device(): pl.pallas_call(copy_kernel, out_shape=shapes, in_specs=[hbm] * 4, out_spe...  2.41 us

profile of v3, /device:TPU:1, one launch (start us, length us, event | category | flops | bytes accessed | tf_op | source)
XLA Modules:
  0.0 53.9 jit_solution(4571944360412136551)
XLA Ops:
  0.6 50.9 %shard_map.111 = (bf16[32,128,128]{2,1,0:T(8,128)(2,1)}, f32[4,32,256]{2,1,0:T(8,128)}, f32[1024,128]{1,0:T(8,128)}, f32[64,256]{1,0:T(8,128)}) custom-call(bf16[4,32,256]{2,1,0:T(8,128)(2,1)} %x_hbm.1, bf16[64,256]{1,0:T(8,128)(2,1)} %bitcast.7, f32[1,256]{1,0:T(1,128)} %bitcast.8, f32[1,256]{1,0:T(1,128)} %bitcast.9, f32[1,64]{1,0:T(1,128)} %bitcast.10, ...), custom_call_target="tpu_custom_call" | custom-call | flops 5000000000 | bytes 4000000 | tf_op jit(solution)/shard_map/pallas_call | solution.py:560
  51.5 2.4 %shard_map.112 = (bf16[32,128,128]{2,1,0:T(8,128)(2,1)}, f32[4,32,256]{2,1,0:T(8,128)}, f32[1024,128]{1,0:T(8,128)}, f32[64,256]{1,0:T(8,128)}) custom-call(bf16[32,128,128]{2,1,0:T(8,128)(2,1)} %get-tuple-element.12.refs_0_, f32[4,32,256]{2,1,0:T(8,128)} %get-tuple-element.13.refs_1_, f32[1024,128]{1,0:T(8,128)} %get-tuple-element.14.refs_2_, ...), custom_call_target="tpu_custom_call" | custom-call | tf_op jit(solution)/shard_map/pallas_call | solution.py:625

commit v4 on v3

v4 whole, which is shorter than its diff:
```python
import functools

import jax
import jax.numpy as jnp
from jax import lax
from jax.experimental import pallas as pl
from jax.experimental.pallas import tpu as pltpu
from jax.sharding import PartitionSpec as P

BF16 = jnp.bfloat16
F32 = jnp.float32
MESH = pl.DeviceIdType.MESH
LANES = 128


def nt(x, y):
    return lax.dot_general(x, y, (((1,), (1,)), ((), ())), preferred_element_type=F32)


def nn(x, y):
    return lax.dot_general(x, y, (((1,), (0,)), ((), ())), preferred_element_type=F32)


def tn(x, y):
    return lax.dot_general(x, y, (((0,), (0,)), ((), ())), preferred_element_type=F32)


def iota(shape, dim):
    return lax.broadcasted_iota(jnp.int32, shape, dim)


def one_hot(cond):
    return jnp.where(cond, 1.0, 0.0).astype(BF16)


def wait_bytes(ref, sem):
    pltpu.make_async_copy(ref, ref, sem).wait()


def lane_aligned(start):
    return pl.multiple_of(start, LANES)


def kernel(
    rows,
    cols,
    x_hbm,
    we_hbm,
    gain_hbm,
    shift_hbm,
    eshift_hbm,
    fshift_hbm,
    wf_hbm,
    g_hbm,
    pair_hbm,
    align_hbm,
    ow_hbm,
    pw_hbm,
    x_ref,
    we_ref,
    gain_ref,
    shift_ref,
    eshift_ref,
    fshift_ref,
    wf_ref,
    a_all,
    ln_all,
    b_all,
    b_piece,
    b_relay,
    gmat,
    wf32,
    w4,
    a_rows_ref,
    held,
    b_t,
    gather_rows,
    scatter_rows,
    aw,
    gp,
    pair_buf,
    align_buf,
    ow_buf,
    pw_buf,
    da_out,
    da_in,
    db_out,
    db_in,
    dw_out,
    dw_in,
    dw_mid,
    dw_fin,
    wg_out,
    wg_in,
    wg_mid,
    wg_fin,
    ready,
    in_sem,
    out_sem,
    send,
    recv,
):
    sl, block, feat = x_ref.shape
    width = we_ref.shape[0] // 2
    ch = wf_ref.shape[1]
    ratio = rows // cols
    seqs = sl * cols
    j_len = ratio * block
    inv_seq = 1.0 / seqs
    inv_res = 1.0 / (rows * block)
    me_r = lax.axis_index("row")
    me_c = lax.axis_index("col")
    near = cols // 2
    nz = rows // near
    y, z = me_r // nz, lax.rem(me_r, nz)
    x, core = me_c // 2, lax.rem(me_c, 2)
    group = near * cols
    member = y * cols + me_c

    ys = [lax.rem(y + k, near) for k in range(near)]
    cs = [lax.rem(me_c + k, cols) for k in range(cols)]
    zs = [lax.rem(z + k, nz) for k in range(nz)]

    def in_ring(k, size):
        return min(k, size - k)

    offsets = sorted(
        ((ky, kc) for ky in range(near) for kc in range(cols) if ky or kc),
        key=lambda o: -(in_ring(o[0], near) + in_ring((o[1] + 1) // 2, near)),
    )
    group_peers = [(ys[ky] * cols + cs[kc], (ys[ky] * nz + z, cs[kc])) for ky, kc in offsets]
    col_peers = [(cs[k], (me_r, cs[k])) for k in range(1, cols)]
    z_peers = [
        (zs[k], (y * nz + zs[k], me_c))
        for k in sorted(range(1, nz), key=lambda k: -in_ring(k, nz))
    ]

    relay_peers = [(x * nz + zs[k], y * 2 + core) for k in (1, nz - 1)]
    chip_peers = [lax.rem(x + k, near) * 2 + core for k in range(1, near)]
    sibling = (me_r, x * 2 + 1 - core)

    def in_group(m):
        return ((m // cols) * nz + z, m % cols)

    def in_z(k):
        return (y * nz + k, me_c)

    barrier = pltpu.get_barrier_semaphore()

    loads = [
        pltpu.make_async_copy(src, dst, in_sem.at[k])
        for k, (src, dst) in enumerate(
            (
                (x_hbm, x_ref),
                (we_hbm, we_ref),
                (gain_hbm, gain_ref),
                (shift_hbm, shift_ref),
                (eshift_hbm, eshift_ref),
                (fshift_hbm, fshift_ref),
                (wf_hbm, wf_ref),
            )
        )
    ]
    for load in loads:
        load.start()
    for device in relay_peers + [device for _, device in z_peers + group_peers]:
        pl.semaphore_signal(barrier, inc=1, device_id=device, device_id_type=MESH)

    for i in range(block):
        pltpu.make_async_copy(
            g_hbm.at[i], gmat.at[:, pl.ds(i * ch, ch)], out_sem.at[0]
        ).start()

    loads[0].wait()
    xf = x_ref[...].astype(F32).reshape(sl * block, feat)
    centre = xf - jnp.mean(xf, axis=-1, keepdims=True)
    inv = lax.rsqrt(jnp.mean(centre * centre, axis=-1, keepdims=True) + 1e-05)
    normed = centre * inv
    for load in loads[1:-1]:
        load.wait()
    gain = gain_ref[...]
    lnout = (normed * gain + shift_ref[...]).astype(BF16)
    ln_all[me_c] = lnout
    we = we_ref[...]
    we4 = jnp.concatenate([we[:width]] * sl + [we[width:]] * sl, axis=0)
    es = eshift_ref[...]
    es4 = jnp.concatenate([es[:, :width]] * sl + [es[:, width:]] * sl, axis=1)
    fshift = fshift_ref[...]
    proj = nt(lnout, we4) + es4
    owner_lane = (iota((block, 2 * LANES), 1) % LANES) // width
    piece = jnp.zeros((block, 2 * LANES), F32)
    for s in range(sl):
        piece = jnp.where(owner_lane == s, proj[s * block : (s + 1) * block], piece)
    piece = piece.astype(BF16)
    a_all[me_c] = piece[:, :LANES]
    b_piece[...] = piece[:, LANES:]

    pl.semaphore_wait(barrier, group - 1 + nz - 1 + 2)

    def remote(src, dst, phase, device, send_phase=None):
        return pltpu.make_async_remote_copy(
            src_ref=src,
            dst_ref=dst,
            send_sem=send.at[phase if send_phase is None else send_phase],
            recv_sem=recv.at[phase],
            device_id=device,
            device_id_type=MESH,
        )

    def to_peers(peers, src, dst, phase):
        for peer, device in peers:
            remote(src(peer), dst, phase, device).start()

    def to_cols(src, dst, phase):
        to_peers(col_peers, src, dst, phase)

    def to_group(src, dst, phase):
        to_peers(group_peers, src, dst, phase)

    def spread(peers, me, device_of, ref, phase):
        for peer in peers:

            @pl.when(me != peer)
            def _():
                remote(ref, ref, phase, device_of(peer)).start()

    group_order = sorted(
        range(group),
        key=lambda m: (in_ring(m // cols, near) + in_ring(m % cols // 2, near), -(m % 2)),
    )
    z_order = sorted(range(nz), key=lambda k: in_ring(k, nz))

    def spread_group(ref, phase):
        spread(group_order, member, in_group, ref, phase)

    def spread_z(ref, phase):
        spread(z_order, z, in_z, ref, phase)

    to_cols(lambda peer: a_all.at[me_c], a_all.at[me_c], 0)
    relays = [
        remote(b_piece, b_relay.at[k], 1, device) for k, device in enumerate(relay_peers)
    ]
    for relay in relays:
        relay.start()

    for _, device in group_peers:
        pl.semaphore_signal(ready, inc=1, device_id=device, device_id_type=MESH)

    loads[-1].wait()
    wf32[...] = wf_ref[...].astype(F32)
    for e in range(width):
        block_e = wf32[pl.ds(e, width, stride=width), :].astype(BF16)
        for s in range(sl):
            w4[s * width : (s + 1) * width, e * ch : (e + 1) * ch] = block_e

    es_len = seqs * width
    is_len = block * seqs
    qi_len = block * cols
    at_row = iota((is_len, qi_len), 0)
    gather_rows[...] = one_hot(
        iota((is_len, qi_len), 1) == ((at_row % seqs) // sl) * block + at_row // seqs
    )
    at_lane = iota((qi_len, is_len), 1)
    scatter_rows[...] = one_hot(
        iota((qi_len, is_len), 0) == ((at_lane % seqs) // sl) * block + at_lane // seqs
    )
    own_seq = iota((is_len, LANES), 0) % sl == iota((is_len, LANES), 1) // width

    wait_bytes(a_all.at[pl.ds(0, cols - 1)], recv.at[0])
    a_cat = a_all[...].reshape(qi_len, LANES)
    a_rows_ref[...] = (jnp.where(own_seq, nn(gather_rows[...], a_cat), 0.0) * inv_seq).astype(
        BF16
    )
    chunk = min(256, is_len)
    lanes = 4 * ch

    def make_aw(m):
        lhs = a_rows_ref[m * chunk : (m + 1) * chunk, :]
        per = chunk // seqs
        for n in range(width // 4):
            res = nn(lhs, w4[:, n * lanes : (n + 1) * lanes]).astype(BF16)
            for el in range(4):
                e = 4 * n + el
                for il in range(per):
                    i = m * per + il
                    aw[e * seqs : (e + 1) * seqs, i * ch : (i + 1) * ch] = res[
                        il * seqs : (il + 1) * seqs, el * ch : (el + 1) * ch
                    ]

    make_aw(0)

    pl.semaphore_wait(ready, group - 1)
    wait_bytes(b_relay, recv.at[1])
    b_from = y * 2 + core
    b_own = []
    for h, z_from in enumerate((zs[nz - 1], zs[1])):
        z_to = [lax.rem(z + nz - core - 2 * h + k, nz) for k in range(4)]
        b_col = x * 2 + z_from // ratio
        b_own.append(b_col == me_c)
        b_slot = pl.ds(pl.multiple_of(lax.rem(z_from, ratio) * block, block), block)
        src, dst = b_relay.at[h], b_all.at[b_from, b_slot]
        for ky in range(near):
            for kz in (3, 0, 2, 1):
                device = (ys[ky] * nz + z_to[kz], b_col)
                plane = remote(src, dst, 2, device, (2, 13)[h])
                if ky or kz not in ((0, 1), (2, 3))[h]:
                    plane.start()
                    continue
                own = jnp.logical_and(z_to[kz] == z, b_own[h])

                @pl.when(jnp.logical_not(own))
                def _():
                    plane.start()

                @pl.when(own)
                def _():
                    pltpu.make_async_copy(src, dst, recv.at[2]).start()

    for col in chip_peers:
        remote(ln_all.at[me_c], ln_all.at[me_c], 11, (me_r, col)).start()
    remote(ln_all.at[me_c], ln_all.at[me_c], 12, sibling).start()

    for m in range(1, is_len // chunk):
        make_aw(m)

    wait_bytes(gmat, out_sem.at[0])
    step = min(512, es_len)
    for n in range(0, es_len, step):
        held[n : n + step, :] = nt(aw[n : n + step, :], gmat[...])
    for q in range(cols):
        rows_q = [held[pl.ds(q * sl + s, width, stride=seqs), :] for s in range(sl)]
        db_out[q] = jnp.concatenate(rows_q, axis=0).T.astype(BF16)

    ks = [lax.rem(me_r // cols + k, ratio) for k in range(ratio)]
    ds = [lax.rem(me_r + k, cols) for k in range(cols)]
    for k_to in ks:
        for col_to in ds:
            row_to = ratio * me_c + k_to
            src = db_out.at[col_to, pl.ds(pl.multiple_of(k_to * block, block), block)]
            own = jnp.logical_and(row_to == me_r, col_to == me_c)

            @pl.when(jnp.logical_not(own))
            def _():
                remote(src, db_in.at[me_r], 3, (row_to, col_to)).start()

            @pl.when(own)
            def _():
                pltpu.make_async_copy(src, db_in.at[me_r], recv.at[3]).start()

    wait_bytes(ln_all.at[pl.ds(0, near - 1)], recv.at[11])
    for col in chip_peers:
        remote(ln_all.at[col], ln_all.at[col], 12, sibling).start()
    wait_bytes(b_all, recv.at[2])
    for q in range(cols):
        held[q * LANES : (q + 1) * LANES, :] = b_all[q].astype(F32).T
    for e in range(width):
        b_t[e * seqs : (e + 1) * seqs, :] = held[pl.ds(e, seqs, stride=width), :].astype(BF16)

    def make_g(m, carry):
        lhs = b_t[pl.ds(pl.multiple_of(m * chunk, chunk), chunk), :]
        per = chunk // seqs
        for n in range(block // 4):
            res = nn(lhs, gmat[:, n * lanes : (n + 1) * lanes]).astype(BF16)
            for il in range(4):
                i = 4 * n + il
                for el in range(per):
                    at = pl.ds(lane_aligned((m * per + el) * ch), ch)
                    gp[i * seqs : (i + 1) * seqs, at] = res[
                        el * seqs : (el + 1) * seqs, il * ch : (il + 1) * ch
                    ]
        return carry

    half = width // 2
    share = width // group
    chunks = es_len // chunk // 2
    for h in range(2):
        lax.fori_loop(h * chunks, (h + 1) * chunks, make_g, 0, unroll=chunks)
        res = tn(a_rows_ref[...], gp[:, h * half * ch : (h + 1) * half * ch])
        res = functools.reduce(
            lambda u, v: u + v, [res[s * width : (s + 1) * width] for s in range(sl)]
        ).astype(BF16)
        for el in range(half):
            dw_out[h * half + el] = res[:, el * ch : (el + 1) * ch]

        for k in range(group // 2):
            peer = h * (group // 2) + lax.rem(member + k, group // 2)

            @pl.when(peer != member)
            def _():
                src = dw_out.at[pl.ds(peer * share, share)]
                remote(src, dw_in.at[member], 5, in_group(peer)).start()

    dw_in[member] = dw_out[pl.ds(member * share, share)]

    step = min(512, is_len)
    da_rows = jnp.concatenate(
        [nt(gp[n : n + step, :], w4[...]) * inv_seq for n in range(0, is_len, step)], axis=0
    )
    da_rows = jnp.where(own_seq, da_rows, 0.0).astype(BF16)
    da_out[...] = nn(scatter_rows[...], da_rows).astype(BF16).reshape(cols, block, LANES)
    wait_bytes(ln_all.at[pl.ds(0, near)], recv.at[12])
    da_cat = da_out[...].reshape(qi_len, LANES)
    wg_a = [
        tn(da_cat, ln_all[:, s * block : (s + 1) * block, :].reshape(qi_len, feat))[
            s * width : (s + 1) * width
        ]
        for s in range(sl)
    ]

    def by_seq(v):
        lane_seq = iota(v.shape, 1) // width
        return jnp.concatenate([jnp.where(lane_seq == s, v, 0.0) for s in range(sl)], axis=0)

    def split(v):
        high = v.astype(BF16)
        return high, (v - high.astype(F32)).astype(BF16)

    wait_bytes(db_in, recv.at[3])
    db_high, db_low = split(by_seq(jnp.sum(db_in[...].astype(F32), axis=0)))
    wg_b = tn(db_high, lnout) + tn(db_low, lnout)
    wg_b = [wg_b[s * width : (s + 1) * width] for s in range(sl)]
    wg = jnp.concatenate([functools.reduce(lambda u, v: u + v, w) for w in (wg_a, wg_b)], axis=0)
    halves = feat // LANES
    part = halves * 2 * width // group
    for h in range(halves):
        for k in range(2 * width // part):
            wg_out[h * 2 * width // part + k] = wg[
                k * part : (k + 1) * part, h * LANES : (h + 1) * LANES
            ]
    to_group(lambda peer: wg_out.at[peer], wg_in.at[member], 8)
    wg_in[member] = wg_out[member]

    to_cols(lambda peer: da_out.at[peer], da_in.at[me_c], 4)
    da_in[me_c] = da_out[me_c]

    b_es = jnp.concatenate(
        [b_t[n : n + LANES, :].T for n in range(0, es_len, LANES)], axis=1
    )
    half = block // 2
    for h in range(2):
        res = nn(b_es, aw[:, h * half * ch : (h + 1) * half * ch])
        for il in range(half):
            pair_buf[h * half + il] = (res[:, il * ch : (il + 1) * ch] + fshift).astype(BF16)
        at = pl.ds(h * half, half)
        pltpu.make_async_copy(pair_buf.at[at], pair_hbm.at[at], out_sem.at[1]).start()

    wait_bytes(dw_in.at[pl.ds(0, group - 1)], recv.at[5])
    dw_mid[z] = jnp.sum(dw_in[...].astype(F32), axis=0).astype(BF16)
    spread_z(dw_mid.at[z], 6)

    wait_bytes(wg_in.at[pl.ds(0, group - 1)], recv.at[8])
    wg_mid[z] = jnp.sum(wg_in[...], axis=0)
    spread_z(wg_mid.at[z], 9)

    wait_bytes(dw_mid.at[pl.ds(0, nz - 1)], recv.at[6])
    dw_fin[member] = (jnp.sum(dw_mid[...].astype(F32), axis=0) * inv_res).astype(BF16)
    spread_group(dw_fin.at[member], 7)

    wait_bytes(da_in.at[pl.ds(0, cols - 1)], recv.at[4])
    da_high, da_low = split(by_seq(jnp.sum(da_in[...].astype(F32), axis=0)))
    dnorm = (
        nn(da_high, we4[:LANES])
        + nn(da_low, we4[:LANES])
        + nn(db_high, we4[LANES:])
        + nn(db_low, we4[LANES:])
    ) * gain
    mean_one = jnp.mean(dnorm, axis=-1, keepdims=True)
    mean_two = jnp.mean(dnorm * normed, axis=-1, keepdims=True)
    align_buf[...] = (inv * (dnorm - mean_one - normed * mean_two)).reshape(sl, block, feat)
    align_copy = pltpu.make_async_copy(align_buf, align_hbm, out_sem.at[2])
    align_copy.start()

    wait_bytes(wg_mid.at[pl.ds(0, nz - 1)], recv.at[9])
    wg_fin[member] = jnp.sum(wg_mid[...], axis=0) * inv_res
    spread_group(wg_fin.at[member], 10)

    wait_bytes(dw_fin.at[pl.ds(0, group - 1)], recv.at[7])
    for m in range(group):
        for k in range(share):
            ow_buf[pl.ds(m * share + k, width, stride=width), :] = dw_fin[m, k].astype(F32)
    ow_copy = pltpu.make_async_copy(ow_buf, ow_hbm, out_sem.at[3])
    ow_copy.start()

    wait_bytes(wg_fin.at[pl.ds(0, group - 1)], recv.at[10])
    for h in range(halves):
        for k in range(2 * width // part):
            pw_buf[k * part : (k + 1) * part, h * LANES : (h + 1) * LANES] = wg_fin[
                h * 2 * width // part + k
            ]
    pw_copy = pltpu.make_async_copy(pw_buf, pw_hbm, out_sem.at[4])
    pw_copy.start()

    wait_bytes(a_all.at[pl.ds(0, cols - 1)], send.at[0])

    wait_bytes(b_relay, send.at[1])
    for phase, own in zip((2, 13), b_own):

        @pl.when(own)
        def _():
            wait_bytes(db_in.at[pl.ds(0, rows // 2 - 1)], send.at[phase])

        @pl.when(jnp.logical_not(own))
        def _():
            wait_bytes(db_in.at[pl.ds(0, rows // 2)], send.at[phase])

    @pl.when(me_r // ratio == me_c)
    def _():
        wait_bytes(db_in.at[pl.ds(0, rows - 1)], send.at[3])

    @pl.when(me_r // ratio != me_c)
    def _():
        wait_bytes(db_in, send.at[3])

    wait_bytes(da_in.at[pl.ds(0, cols - 1)], send.at[4])
    wait_bytes(dw_in.at[pl.ds(0, group - 1)], send.at[5])
    wait_bytes(dw_mid.at[pl.ds(0, nz - 1)], send.at[6])
    wait_bytes(dw_fin.at[pl.ds(0, group - 1)], send.at[7])
    wait_bytes(wg_in.at[pl.ds(0, group - 1)], send.at[8])
    wait_bytes(wg_mid.at[pl.ds(0, nz - 1)], send.at[9])
    wait_bytes(wg_fin.at[pl.ds(0, group - 1)], send.at[10])
    wait_bytes(ln_all.at[pl.ds(0, near - 1)], send.at[11])
    wait_bytes(ln_all.at[pl.ds(0, near)], send.at[12])
    wait_bytes(pair_buf, out_sem.at[1])
    align_copy.wait()
    ow_copy.wait()
    pw_copy.wait()


def copy_kernel(*refs):
    sem = refs[8]
    copies = [pltpu.make_async_copy(refs[k], refs[4 + k], sem.at[k]) for k in range(4)]
    for copy in copies:
        copy.start()
    for copy in copies:
        copy.wait()


def on_device(x, gain, shift, we, eshift, wf, fshift, g):
    rows = lax.axis_size("row")
    cols = lax.axis_size("col")
    sl, block, feat = x.shape
    width = we.shape[1] // 2
    ch = wf.shape[1]
    j_len = g.shape[1]
    seqs = sl * cols
    near = cols // 2
    nz = rows // near
    group = near * cols
    share = width // group
    part = feat * 2 * width // LANES // group
    hbm = pl.BlockSpec(memory_space=pl.ANY)

    def buf(*shape, dtype=BF16):
        return pltpu.VMEM(shape, dtype)

    shapes = [
        jax.ShapeDtypeStruct((block, j_len, ch), BF16),
        jax.ShapeDtypeStruct((sl, block, feat), F32),
        jax.ShapeDtypeStruct((width * width, ch), F32),
        jax.ShapeDtypeStruct((2 * width, feat), F32),
    ]
    outs = pl.pallas_call(
        functools.partial(kernel, rows, cols),
        out_shape=shapes,
        in_specs=[hbm] * 8,
        out_specs=[hbm] * 4,
        scratch_shapes=[
            buf(sl, block, feat),
            buf(2 * width, feat),
            buf(1, feat, dtype=F32),
            buf(1, feat, dtype=F32),
            buf(1, 2 * width, dtype=F32),
            buf(1, ch, dtype=F32),
            buf(width * width, ch),
            buf(cols, block, LANES),
            buf(cols, sl * block, feat),
            buf(cols, j_len, LANES),
            buf(block, LANES),
            buf(2, block, LANES),
            buf(j_len, block * ch),
            buf(width * width, ch, dtype=F32),
            buf(LANES, width * ch),
            buf(block * seqs, LANES),
            buf(seqs * width, j_len, dtype=F32),
            buf(seqs * width, j_len),
            buf(block * seqs, cols * block),
            buf(cols * block, block * seqs),
            buf(width * seqs, block * ch),
            buf(block * seqs, width * ch),
            buf(block, j_len, ch),
            buf(sl, block, feat, dtype=F32),
            buf(width * width, ch, dtype=F32),
            buf(2 * width, feat, dtype=F32),
            buf(cols, block, LANES),
            buf(cols, block, LANES),
            buf(cols, j_len, LANES),
            buf(rows, block, LANES),
            buf(width, width, ch),
            buf(group, share, width, ch),
            buf(nz, share, width, ch),
            buf(group, share, width, ch),
            buf(group, part, LANES, dtype=F32),
            buf(group, part, LANES, dtype=F32),
            buf(nz, part, LANES, dtype=F32),
            buf(group, part, LANES, dtype=F32),
            pltpu.SemaphoreType.REGULAR,
            pltpu.SemaphoreType.DMA((7,)),
            pltpu.SemaphoreType.DMA((5,)),
            pltpu.SemaphoreType.DMA((14,)),
            pltpu.SemaphoreType.DMA((14,)),
        ],
        compiler_params=pltpu.CompilerParams(
            collective_id=0, has_side_effects=True, vmem_limit_bytes=34 * 1024 * 1024
        ),
        cost_estimate=pl.CostEstimate(
            flops=5_000_000_000, bytes_accessed=4_000_000, transcendentals=0
        ),
    )(
        *(
            pltpu.with_memory_space_constraint(v, pltpu.HBM)
            for v in (
                x,
                we.T,
                gain.reshape(1, feat),
                shift.reshape(1, feat),
                eshift.reshape(1, 2 * width),
                fshift.reshape(1, ch),
                wf,
                g,
            )
        )
    )
    pair, align, ow, pw = pl.pallas_call(
        copy_kernel,
        out_shape=shapes,
        in_specs=[hbm] * 4,
        out_specs=[hbm] * 4,
        scratch_shapes=[pltpu.SemaphoreType.DMA((4,))],
        compiler_params=pltpu.CompilerParams(vmem_limit_bytes=16 * 1024 * 1024),
    )(*outs)
    return pair, align, ow, pw.T


def solution(mesh):
    in_specs = (P("col", "row", None), P(), P(), P(), P(), P(), P(), P("row", "col", None))
    out_specs = (P("row", "col", None), P("col", "row", None), P(), P())
    return jax.shard_map(
        on_device, mesh=mesh, in_specs=in_specs, out_specs=out_specs, check_vma=False
    )
```

time: 54 us -> 48.5 us (0.90)
  Pallas kernels: 53.3 us -> 47.6 us
    pallas_call x1, Pallas kernels: 50.9 us -> 46.4 us  [on_device(): pl.pallas_call(functools.partial(kernel, rows, cols), out_shape=shapes, i...]
    pallas_call x1, Pallas kernels: 2.41 us -> 1.23 us  [on_device(): pl.pallas_call(copy_kernel, out_shape=shapes, in_specs=[hbm] * 4, out_spe...]
where the time goes in v4:
time: 48.5 us; the launch traced here: 48.4 us
  Pallas kernels  47.6 us (98%)
  between operations  0.8 us (2%)
    pallas_call x1, Pallas kernels, on_device(): pl.pallas_call(functools.partial(kernel, rows, cols), out_shape=shapes, i...  46.4 us
    pallas_call x1, Pallas kernels, on_device(): pl.pallas_call(copy_kernel, out_shape=shapes, in_specs=[hbm] * 4, out_spe...  1.23 us

profile of v4, /device:TPU:1, one launch (start us, length us, event | category | flops | bytes accessed | tf_op | source)
XLA Modules:
  0.0 48.4 jit_solution(760026839527082018)
XLA Ops:
  0.6 46.4 %shard_map.111 = (bf16[32,128,128]{2,1,0:T(8,128)(2,1)S(1)}, f32[4,32,256]{2,1,0:T(8,128)S(1)}, f32[1024,128]{1,0:T(8,128)S(1)}, f32[64,256]{1,0:T(8,128)S(1)}) custom-call(bf16[4,32,256]{2,1,0:T(8,128)(2,1)} %x_hbm.1, bf16[64,256]{1,0:T(8,128)(2,1)} %bitcast.7, f32[1,256]{1,0:T(1,128)} %bitcast.8, f32[1,256]{1,0:T(1,128)} %bitcast.9, f32[1,64]{1,0:T(1,128)} %bitcast.10, ...), custom_call_target="tpu_custom_call" | custom-call | flops 5000000000 | bytes 4000000 | tf_op jit(solution)/shard_map/pallas_call | solution.py:562
  47.0 1.2 %shard_map.112 = (bf16[32,128,128]{2,1,0:T(8,128)(2,1)}, f32[4,32,256]{2,1,0:T(8,128)}, f32[1024,128]{1,0:T(8,128)}, f32[64,256]{1,0:T(8,128)}) custom-call(bf16[32,128,128]{2,1,0:T(8,128)(2,1)S(1)} %get-tuple-element.12.refs_0_, f32[4,32,256]{2,1,0:T(8,128)S(1)} %get-tuple-element.13.refs_1_, f32[1024,128]{1,0:T(8,128)S(1)} %get-tuple-element.14.refs_2_, ...), custom_call_target="tpu_custom_call" | custom-call | tf_op jit(solution)/shard_map/pallas_call | solution.py:633

commit v5 on v4

--- a/solution.py
+++ b/solution.py
@@ -65,6 +65,7 @@
     wf_ref,
     a_all,
     ln_all,
+    ln_relay,
     b_all,
     b_piece,
     b_relay,
@@ -86,6 +87,8 @@
     da_in,
     db_out,
     db_in,
+    db_sum,
+    db_fin,
     dw_out,
     dw_in,
     dw_mid,
@@ -137,6 +140,7 @@
 
     relay_peers = [(x * nz + zs[k], y * 2 + core) for k in (1, nz - 1)]
     chip_peers = [lax.rem(x + k, near) * 2 + core for k in range(1, near)]
+    z_near = [(y * nz + zs[k], me_c) for k in (1, nz - 1)]
     sibling = (me_r, x * 2 + 1 - core)
 
     def in_group(m):
@@ -236,12 +240,12 @@
     def spread_z(ref, phase):
         spread(z_order, z, in_z, ref, phase)
 
-    to_cols(lambda peer: a_all.at[me_c], a_all.at[me_c], 0)
     relays = [
         remote(b_piece, b_relay.at[k], 1, device) for k, device in enumerate(relay_peers)
     ]
     for relay in relays:
         relay.start()
+    to_cols(lambda peer: a_all.at[me_c], a_all.at[me_c], 0)
 
     for _, device in group_peers:
         pl.semaphore_signal(ready, inc=1, device_id=device, device_id_type=MESH)
@@ -299,7 +303,7 @@
         b_own.append(b_col == me_c)
         b_slot = pl.ds(pl.multiple_of(lax.rem(z_from, ratio) * block, block), block)
         src, dst = b_relay.at[h], b_all.at[b_from, b_slot]
-        for ky in range(near):
+        for ky in sorted(range(near), key=lambda k: -in_ring(k, near)):
             for kz in (3, 0, 2, 1):
                 device = (ys[ky] * nz + z_to[kz], b_col)
                 plane = remote(src, dst, 2, device, (2, 13)[h])
@@ -331,21 +335,32 @@
         rows_q = [held[pl.ds(q * sl + s, width, stride=seqs), :] for s in range(sl)]
         db_out[q] = jnp.concatenate(rows_q, axis=0).T.astype(BF16)
 
-    ks = [lax.rem(me_r // cols + k, ratio) for k in range(ratio)]
-    ds = [lax.rem(me_r + k, cols) for k in range(cols)]
-    for k_to in ks:
-        for col_to in ds:
-            row_to = ratio * me_c + k_to
-            src = db_out.at[col_to, pl.ds(pl.multiple_of(k_to * block, block), block)]
-            own = jnp.logical_and(row_to == me_r, col_to == me_c)
-
-            @pl.when(jnp.logical_not(own))
-            def _():
-                remote(src, db_in.at[me_r], 3, (row_to, col_to)).start()
-
-            @pl.when(own)
-            def _():
-                pltpu.make_async_copy(src, db_in.at[me_r], recv.at[3]).start()
+    for k in range(ratio):
+        k_to = lax.rem(y + k, ratio)
+        z_own = ratio * core + k_to
+        for kc in range(2):
+            c_to = lax.rem(kc + z // ratio, 2)
+            turn = lax.rem(z - z_own - 1 + c_to + 2 * nz, nz)
+            z_relay = lax.rem(z_own + 1 - 2 * (turn // 4) + nz, nz)
+            for kx in range(near):
+                x_to = lax.rem(x + z + kx, near)
+                src = db_out.at[
+                    x_to * 2 + c_to, pl.ds(pl.multiple_of(k_to * block, block), block)
+                ]
+                dst = db_in.at[turn * near + y]
+                device = (x * nz + z_relay, x_to * 2 + c_to)
+                own = jnp.logical_and(device[0] == me_r, device[1] == me_c)
+
+                @pl.when(jnp.logical_not(own))
+                def _():
+                    remote(src, dst, 3, device).start()
+
+                @pl.when(own)
+                def _():
+                    pltpu.make_async_copy(src, dst, recv.at[3]).start()
+
+    for h, device in enumerate(z_near):
+        remote(ln_all.at[me_c], ln_relay.at[h], 15, device).start()
 
     wait_bytes(ln_all.at[pl.ds(0, near - 1)], recv.at[11])
     for col in chip_peers:
@@ -416,8 +431,12 @@
         return high, (v - high.astype(F32)).astype(BF16)
 
     wait_bytes(db_in, recv.at[3])
-    db_high, db_low = split(by_seq(jnp.sum(db_in[...].astype(F32), axis=0)))
-    wg_b = tn(db_high, lnout) + tn(db_low, lnout)
+    wait_bytes(ln_relay, recv.at[15])
+    wg_b = 0.0
+    for h in range(2):
+        db = jnp.sum(db_in[h * (rows // 2) : (h + 1) * (rows // 2)].astype(F32), axis=0)
+        db_sum[h] = db.astype(BF16)
+        wg_b += tn(by_seq(db).astype(BF16), ln_relay[h])
     wg_b = [wg_b[s * width : (s + 1) * width] for s in range(sl)]
     wg = jnp.concatenate([functools.reduce(lambda u, v: u + v, w) for w in (wg_a, wg_b)], axis=0)
     halves = feat // LANES
@@ -432,6 +451,8 @@
 
     to_cols(lambda peer: da_out.at[peer], da_in.at[me_c], 4)
     da_in[me_c] = da_out[me_c]
+    for h in range(2):
+        remote(db_sum.at[h], db_fin.at[h], 16, z_near[1 - h]).start()
 
     b_es = jnp.concatenate(
         [b_t[n : n + LANES, :].T for n in range(0, es_len, LANES)], axis=1
@@ -453,10 +474,18 @@
     spread_z(wg_mid.at[z], 9)
 
     wait_bytes(dw_mid.at[pl.ds(0, nz - 1)], recv.at[6])
-    dw_fin[member] = (jnp.sum(dw_mid[...].astype(F32), axis=0) * inv_res).astype(BF16)
-    spread_group(dw_fin.at[member], 7)
+    dw_fin[core, member // 2] = (jnp.sum(dw_mid[...].astype(F32), axis=0) * inv_res).astype(BF16)
+    for chip in range(group // 2):
+
+        @pl.when(member // 2 != chip)
+        def _():
+            own_part = dw_fin.at[core, member // 2]
+            remote(own_part, own_part, 7, in_group(2 * chip + core)).start()
+
 
     wait_bytes(da_in.at[pl.ds(0, cols - 1)], recv.at[4])
+    wait_bytes(db_fin, recv.at[16])
+    db_high, db_low = split(by_seq(jnp.sum(db_fin[...].astype(F32), axis=0)))
     da_high, da_low = split(by_seq(jnp.sum(da_in[...].astype(F32), axis=0)))
     dnorm = (
         nn(da_high, we4[:LANES])
@@ -474,10 +503,20 @@
     wg_fin[member] = jnp.sum(wg_mid[...], axis=0) * inv_res
     spread_group(wg_fin.at[member], 10)
 
-    wait_bytes(dw_fin.at[pl.ds(0, group - 1)], recv.at[7])
-    for m in range(group):
-        for k in range(share):
-            ow_buf[pl.ds(m * share + k, width, stride=width), :] = dw_fin[m, k].astype(F32)
+    wait_bytes(dw_fin.at[0, pl.ds(0, group // 2 - 1)], recv.at[7])
+    remote(dw_fin.at[core], dw_fin.at[core], 14, sibling).start()
+
+    def put_dw(half):
+        for chip in range(group // 2):
+            for k in range(share):
+                at = pl.ds((2 * chip + half) * share + k, width, stride=width)
+                ow_buf[at, :] = dw_fin[half, chip, k].astype(F32)
+
+    for half in range(2):
+        pl.when(core == half)(functools.partial(put_dw, half))
+    wait_bytes(dw_fin.at[0], recv.at[14])
+    for half in range(2):
+        pl.when(core != half)(functools.partial(put_dw, half))
     ow_copy = pltpu.make_async_copy(ow_buf, ow_hbm, out_sem.at[3])
     ow_copy.start()
 
@@ -503,18 +542,22 @@
         def _():
             wait_bytes(db_in.at[pl.ds(0, rows // 2)], send.at[phase])
 
-    @pl.when(me_r // ratio == me_c)
-    def _():
-        wait_bytes(db_in.at[pl.ds(0, rows - 1)], send.at[3])
-
-    @pl.when(me_r // ratio != me_c)
-    def _():
-        wait_bytes(db_in, send.at[3])
-
+    own_count = jnp.where(
+        x == y, b_own[0].astype(jnp.int32) + b_own[1].astype(jnp.int32), 0
+    )
+    for k in range(3):
+
+        @pl.when(own_count == k)
+        def _():
+            wait_bytes(db_in.at[pl.ds(0, rows - k)], send.at[3])
+
+    wait_bytes(ln_relay, send.at[15])
+    wait_bytes(db_fin, send.at[16])
     wait_bytes(da_in.at[pl.ds(0, cols - 1)], send.at[4])
     wait_bytes(dw_in.at[pl.ds(0, group - 1)], send.at[5])
     wait_bytes(dw_mid.at[pl.ds(0, nz - 1)], send.at[6])
-    wait_bytes(dw_fin.at[pl.ds(0, group - 1)], send.at[7])
+    wait_bytes(dw_fin.at[0, pl.ds(0, group // 2 - 1)], send.at[7])
+    wait_bytes(dw_fin.at[0], send.at[14])
     wait_bytes(wg_in.at[pl.ds(0, group - 1)], send.at[8])
     wait_bytes(wg_mid.at[pl.ds(0, nz - 1)], send.at[9])
     wait_bytes(wg_fin.at[pl.ds(0, group - 1)], send.at[10])
@@ -574,6 +617,7 @@
             buf(width * width, ch),
             buf(cols, block, LANES),
             buf(cols, sl * block, feat),
+            buf(2, sl * block, feat),
             buf(cols, j_len, LANES),
             buf(block, LANES),
             buf(2, block, LANES),
@@ -595,10 +639,12 @@
             buf(cols, block, LANES),
             buf(cols, j_len, LANES),
             buf(rows, block, LANES),
+            buf(2, block, LANES),
+            buf(2, block, LANES),
             buf(width, width, ch),
             buf(group, share, width, ch),
             buf(nz, share, width, ch),
-            buf(group, share, width, ch),
+            buf(2, group // 2, share, width, ch),
             buf(group, part, LANES, dtype=F32),
             buf(group, part, LANES, dtype=F32),
             buf(nz, part, LANES, dtype=F32),
@@ -606,8 +652,8 @@
             pltpu.SemaphoreType.REGULAR,
             pltpu.SemaphoreType.DMA((7,)),
             pltpu.SemaphoreType.DMA((5,)),
-            pltpu.SemaphoreType.DMA((14,)),
-            pltpu.SemaphoreType.DMA((14,)),
+            pltpu.SemaphoreType.DMA((17,)),
+            pltpu.SemaphoreType.DMA((17,)),
         ],
         compiler_params=pltpu.CompilerParams(
             collective_id=0, has_side_effects=True, vmem_limit_bytes=34 * 1024 * 1024

time: 48.5 us -> 46.5 us (0.959)
  Pallas kernels: 47.6 us -> 45.6 us
    pallas_call x1, Pallas kernels: 46.4 us -> 44.4 us  [on_device(): pl.pallas_call(functools.partial(kernel, rows, cols), out_shape=shapes, i...]
where the time goes in v5:
time: 46.5 us; the launch traced here: 46.4 us
  Pallas kernels  45.6 us (98%)
  between operations  0.8 us (2%)
    pallas_call x1, Pallas kernels, on_device(): pl.pallas_call(functools.partial(kernel, rows, cols), out_shape=shapes, i...  44.4 us
    pallas_call x1, Pallas kernels, on_device(): pl.pallas_call(copy_kernel, out_shape=shapes, in_specs=[hbm] * 4, out_spe...  1.23 us

profile of v5, /device:TPU:1, one launch (start us, length us, event | category | flops | bytes accessed | tf_op | source)
XLA Modules:
  0.0 46.4 jit_solution(2382091191774148687)
XLA Ops:
  0.6 44.4 %shard_map.111 = (bf16[32,128,128]{2,1,0:T(8,128)(2,1)S(1)}, f32[4,32,256]{2,1,0:T(8,128)S(1)}, f32[1024,128]{1,0:T(8,128)S(1)}, f32[64,256]{1,0:T(8,128)S(1)}) custom-call(bf16[4,32,256]{2,1,0:T(8,128)(2,1)} %x_hbm.1, bf16[64,256]{1,0:T(8,128)(2,1)} %bitcast.7, f32[1,256]{1,0:T(1,128)} %bitcast.8, f32[1,256]{1,0:T(1,128)} %bitcast.9, f32[1,64]{1,0:T(1,128)} %bitcast.10, ...), custom_call_target="tpu_custom_call" | custom-call | flops 5000000000 | bytes 4000000 | tf_op jit(solution)/shard_map/pallas_call | solution.py:605
  45.0 1.2 %shard_map.112 = (bf16[32,128,128]{2,1,0:T(8,128)(2,1)}, f32[4,32,256]{2,1,0:T(8,128)}, f32[1024,128]{1,0:T(8,128)}, f32[64,256]{1,0:T(8,128)}) custom-call(bf16[32,128,128]{2,1,0:T(8,128)(2,1)S(1)} %get-tuple-element.12.refs_0_, f32[4,32,256]{2,1,0:T(8,128)S(1)} %get-tuple-element.13.refs_1_, f32[1024,128]{1,0:T(8,128)S(1)} %get-tuple-element.14.refs_2_, ...), custom_call_target="tpu_custom_call" | custom-call | tf_op jit(solution)/shard_map/pallas_call | solution.py:679

commit v6 on v5

--- a/solution.py
+++ b/solution.py
@@ -138,7 +138,13 @@
         for k in sorted(range(1, nz), key=lambda k: -in_ring(k, nz))
     ]
 
-    relay_peers = [(x * nz + zs[k], y * 2 + core) for k in (1, nz - 1)]
+    turned = [lax.rem(v + near // 2, near) for v in (x, y)]
+    relay_peers = [
+        (v * nz + zs[k], y * 2 + core) for v in (x, turned[0]) for k in (1, nz - 1)
+    ]
+    relay_sources = [
+        (x * nz + zs[k], v * 2 + core) for v in (y, turned[1]) for k in (1, nz - 1)
+    ]
     chip_peers = [lax.rem(x + k, near) * 2 + core for k in range(1, near)]
     z_near = [(y * nz + zs[k], me_c) for k in (1, nz - 1)]
     sibling = (me_r, x * 2 + 1 - core)
@@ -165,10 +171,12 @@
             )
         )
     ]
-    for load in loads:
+    loads[0].start()
+    loads[1].start()
+    for device in relay_sources + [device for _, device in z_peers + group_peers]:
+        pl.semaphore_signal(barrier, inc=1, device_id=device, device_id_type=MESH)
+    for load in loads[2:]:
         load.start()
-    for device in relay_peers + [device for _, device in z_peers + group_peers]:
-        pl.semaphore_signal(barrier, inc=1, device_id=device, device_id_type=MESH)
 
     for i in range(block):
         pltpu.make_async_copy(
@@ -199,7 +207,7 @@
     a_all[me_c] = piece[:, :LANES]
     b_piece[...] = piece[:, LANES:]
 
-    pl.semaphore_wait(barrier, group - 1 + nz - 1 + 2)
+    pl.semaphore_wait(barrier, group - 1 + nz - 1 + 4)
 
     def remote(src, dst, phase, device, send_phase=None):
         return pltpu.make_async_remote_copy(
@@ -240,12 +248,12 @@
     def spread_z(ref, phase):
         spread(z_order, z, in_z, ref, phase)
 
+    to_cols(lambda peer: a_all.at[me_c], a_all.at[me_c], 0)
     relays = [
         remote(b_piece, b_relay.at[k], 1, device) for k, device in enumerate(relay_peers)
     ]
     for relay in relays:
         relay.start()
-    to_cols(lambda peer: a_all.at[me_c], a_all.at[me_c], 0)
 
     for _, device in group_peers:
         pl.semaphore_signal(ready, inc=1, device_id=device, device_id_type=MESH)
@@ -295,30 +303,31 @@
 
     pl.semaphore_wait(ready, group - 1)
     wait_bytes(b_relay, recv.at[1])
-    b_from = y * 2 + core
     b_own = []
+    y_to = [y, lax.rem(y + 1 + 2 * core, near)]
     for h, z_from in enumerate((zs[nz - 1], zs[1])):
         z_to = [lax.rem(z + nz - core - 2 * h + k, nz) for k in range(4)]
         b_col = x * 2 + z_from // ratio
         b_own.append(b_col == me_c)
         b_slot = pl.ds(pl.multiple_of(lax.rem(z_from, ratio) * block, block), block)
-        src, dst = b_relay.at[h], b_all.at[b_from, b_slot]
-        for ky in sorted(range(near), key=lambda k: -in_ring(k, near)):
+        for ky in (1, 0):
             for kz in (3, 0, 2, 1):
-                device = (ys[ky] * nz + z_to[kz], b_col)
-                plane = remote(src, dst, 2, device, (2, 13)[h])
-                if ky or kz not in ((0, 1), (2, 3))[h]:
-                    plane.start()
-                    continue
-                own = jnp.logical_and(z_to[kz] == z, b_own[h])
-
-                @pl.when(jnp.logical_not(own))
-                def _():
-                    plane.start()
-
-                @pl.when(own)
-                def _():
-                    pltpu.make_async_copy(src, dst, recv.at[2]).start()
+                for v, x_from in enumerate((y, turned[1])):
+                    src, dst = b_relay.at[2 * v + h], b_all.at[x_from * 2 + core, b_slot]
+                    device = (y_to[ky] * nz + z_to[kz], b_col)
+                    plane = remote(src, dst, 2, device, (2, 13)[h])
+                    if ky or kz not in ((0, 1), (2, 3))[h]:
+                        plane.start()
+                        continue
+                    own = jnp.logical_and(z_to[kz] == z, b_own[h])
+
+                    @pl.when(jnp.logical_not(own))
+                    def _():
+                        plane.start()
+
+                    @pl.when(own)
+                    def _():
+                        pltpu.make_async_copy(src, dst, recv.at[2]).start()
 
     for col in chip_peers:
         remote(ln_all.at[me_c], ln_all.at[me_c], 11, (me_r, col)).start()
@@ -449,6 +458,10 @@
     to_group(lambda peer: wg_out.at[peer], wg_in.at[member], 8)
     wg_in[member] = wg_out[member]
 
+    wait_bytes(dw_in.at[pl.ds(0, group - 1)], recv.at[5])
+    dw_mid[z] = jnp.sum(dw_in[...].astype(F32), axis=0).astype(BF16)
+    spread_z(dw_mid.at[z], 6)
+
     to_cols(lambda peer: da_out.at[peer], da_in.at[me_c], 4)
     da_in[me_c] = da_out[me_c]
     for h in range(2):
@@ -464,10 +477,6 @@
             pair_buf[h * half + il] = (res[:, il * ch : (il + 1) * ch] + fshift).astype(BF16)
         at = pl.ds(h * half, half)
         pltpu.make_async_copy(pair_buf.at[at], pair_hbm.at[at], out_sem.at[1]).start()
-
-    wait_bytes(dw_in.at[pl.ds(0, group - 1)], recv.at[5])
-    dw_mid[z] = jnp.sum(dw_in[...].astype(F32), axis=0).astype(BF16)
-    spread_z(dw_mid.at[z], 6)
 
     wait_bytes(wg_in.at[pl.ds(0, group - 1)], recv.at[8])
     wg_mid[z] = jnp.sum(wg_in[...], axis=0)
@@ -520,15 +529,6 @@
     ow_copy = pltpu.make_async_copy(ow_buf, ow_hbm, out_sem.at[3])
     ow_copy.start()
 
-    wait_bytes(wg_fin.at[pl.ds(0, group - 1)], recv.at[10])
-    for h in range(halves):
-        for k in range(2 * width // part):
-            pw_buf[k * part : (k + 1) * part, h * LANES : (h + 1) * LANES] = wg_fin[
-                h * 2 * width // part + k
-            ]
-    pw_copy = pltpu.make_async_copy(pw_buf, pw_hbm, out_sem.at[4])
-    pw_copy.start()
-
     wait_bytes(a_all.at[pl.ds(0, cols - 1)], send.at[0])
 
     wait_bytes(b_relay, send.at[1])
@@ -536,7 +536,7 @@
 
         @pl.when(own)
         def _():
-            wait_bytes(db_in.at[pl.ds(0, rows // 2 - 1)], send.at[phase])
+            wait_bytes(db_in.at[pl.ds(0, rows // 2 - 2)], send.at[phase])
 
         @pl.when(jnp.logical_not(own))
         def _():
@@ -560,14 +560,23 @@
     wait_bytes(dw_fin.at[0], send.at[14])
     wait_bytes(wg_in.at[pl.ds(0, group - 1)], send.at[8])
     wait_bytes(wg_mid.at[pl.ds(0, nz - 1)], send.at[9])
-    wait_bytes(wg_fin.at[pl.ds(0, group - 1)], send.at[10])
     wait_bytes(ln_all.at[pl.ds(0, near - 1)], send.at[11])
     wait_bytes(ln_all.at[pl.ds(0, near)], send.at[12])
     wait_bytes(pair_buf, out_sem.at[1])
     align_copy.wait()
     ow_copy.wait()
+
+    wait_bytes(wg_fin.at[pl.ds(0, group - 1)], recv.at[10])
+    for h in range(halves):
+        for k in range(2 * width // part):
+            pw_buf[k * part : (k + 1) * part, h * LANES : (h + 1) * LANES] = wg_fin[
+                h * 2 * width // part + k
+            ]
+    pw_copy = pltpu.make_async_copy(pw_buf, pw_hbm, out_sem.at[4])
+    pw_copy.start()
+
+    wait_bytes(wg_fin.at[pl.ds(0, group - 1)], send.at[10])
     pw_copy.wait()
-
 
 def copy_kernel(*refs):
     sem = refs[8]
@@ -620,7 +629,7 @@
             buf(2, sl * block, feat),
             buf(cols, j_len, LANES),
             buf(block, LANES),
-            buf(2, block, LANES),
+            buf(4, block, LANES),
             buf(j_len, block * ch),
             buf(width * width, ch, dtype=F32),
             buf(LANES, width * ch),

time: 46.5 us -> 46.5 us (level)
  no operation moved by 1% of the time
where the time goes in v6:
time: 46.5 us; the launch traced here: 46.3 us
  Pallas kernels  45.5 us (98%)
  between operations  0.8 us (2%)
    pallas_call x1, Pallas kernels, on_device(): pl.pallas_call(functools.partial(kernel, rows, cols), out_shape=shapes, i...  44.3 us
    pallas_call x1, Pallas kernels, on_device(): pl.pallas_call(copy_kernel, out_shape=shapes, in_specs=[hbm] * 4, out_spe...  1.23 us

profile of v6, /device:TPU:1, one launch (start us, length us, event | category | flops | bytes accessed | tf_op | source)
XLA Modules:
  0.0 46.3 jit_solution(9455020849472050492)
XLA Ops:
  0.6 44.3 %shard_map.111 = (bf16[32,128,128]{2,1,0:T(8,128)(2,1)S(1)}, f32[4,32,256]{2,1,0:T(8,128)S(1)}, f32[1024,128]{1,0:T(8,128)S(1)}, f32[64,256]{1,0:T(8,128)S(1)}) custom-call(bf16[4,32,256]{2,1,0:T(8,128)(2,1)} %x_hbm.1, bf16[64,256]{1,0:T(8,128)(2,1)} %bitcast.7, f32[1,256]{1,0:T(1,128)} %bitcast.8, f32[1,256]{1,0:T(1,128)} %bitcast.9, f32[1,64]{1,0:T(1,128)} %bitcast.10, ...), custom_call_target="tpu_custom_call" | custom-call | flops 5000000000 | bytes 4000000 | tf_op jit(solution)/shard_map/pallas_call | solution.py:614
  44.9 1.2 %shard_map.112 = (bf16[32,128,128]{2,1,0:T(8,128)(2,1)}, f32[4,32,256]{2,1,0:T(8,128)}, f32[1024,128]{1,0:T(8,128)}, f32[64,256]{1,0:T(8,128)}) custom-call(bf16[32,128,128]{2,1,0:T(8,128)(2,1)S(1)} %get-tuple-element.12.refs_0_, f32[4,32,256]{2,1,0:T(8,128)S(1)} %get-tuple-element.13.refs_1_, f32[1024,128]{1,0:T(8,128)S(1)} %get-tuple-element.14.refs_2_, ...), custom_call_target="tpu_custom_call" | custom-call | tf_op jit(solution)/shard_map/pallas_call | solution.py:688
